TPU v7x, 32 devices: a whole 2x2x4 slice. The times are simulated.
32 devices in a mesh: ctx: 16 (over z, x, core), head: 2 (over y).
Axes of the slice: x: 2, y: 2, z: 4, core: 2. Of those that a mesh axis runs over, the one named last changes fastest.
Arguments:
- inputs: bfloat16 [5120, 3072], P('ctx', 'head'), may hold values from -6 to 6
- norm_gain: float32 [3072], replicated, may hold values from 0.1 to 1.9
- level_table: bfloat16 [8, 3072], replicated, may hold values from -6 to 6
- w_qkv: bfloat16 [3072, 3, 3072], P(None, None, 'head'), may hold values from -4 to 4
- w_out: bfloat16 [3072, 3072], P('head'), may hold values from -0.21875 to 0.21875
- clip_lengths: int32 [8], replicated, may hold values from 1 to 2560, 5120 in all
- prefix_lengths: int32 [8], replicated, may hold values from 1 to 640
- noise_levels: int32 [8], replicated, may hold values from 0 to 7
- token_rank: int32 [5120], replicated, may hold values from 0 to 15, as said below
Outputs:
- attended: bfloat16 [5120, 3072], P('ctx', 'head')
Inputs may be any that keep to these rules, and one draw needn't show every extreme that they name: `clip_lengths`: they sum to 5120; the longest clip has exactly 2560 tokens. `token_rank`: every rank receives exactly 320 tokens. Every block of 320 packed rows gives the same number of tokens to the rank k places after its own index (counted around 16), for each k; no block gives more than 40 tokens to one rank, and that number is reached.
All inputs are finite; a program needn't handle non-finite values.
Results may differ from a plain program's by a relative error of at most 0.009.
Values may be sent and summed in bfloat16 or wider, within the bound.
No kernel may reach another device: no remote copies, remote signals or barrier semaphores. Data moves between devices by JAX's collectives and lax.ppermute only.
A program may use at most 384 MiB of HBM per device.

v0:
```python
import jax
import jax.numpy as jnp
from jax import lax
from jax.sharding import PartitionSpec as P

HEAD_DIM = 128


NEG = -1e30
EPS = 1e-06


def clip_tables(total_rows, clip_lengths, prefix_lengths, noise_levels):
    rows = jnp.arange(total_rows, dtype=jnp.int32)
    ends = jnp.cumsum(clip_lengths)
    begins = ends - clip_lengths
    clip_of = jnp.sum((rows[:, None] >= ends[None, :]).astype(jnp.int32), axis=1)
    member = clip_of[:, None] == jnp.arange(clip_lengths.shape[0], dtype=jnp.int32)[None, :]
    begin_row = jnp.sum(jnp.where(member, begins[None, :], 0), axis=1)
    lead = jnp.minimum(prefix_lengths, clip_lengths)
    lead_row = jnp.sum(jnp.where(member, lead[None, :], 0), axis=1)
    level_row = jnp.sum(jnp.where(member, noise_levels[None, :], 0), axis=1)
    in_prefix = rows - begin_row < lead_row
    return (clip_of, in_prefix, level_row)


def rank_tables(token_rank, ranks, per_rank):
    onehot = (token_rank[:, None] == jnp.arange(ranks, dtype=jnp.int32)[None, :]).astype(jnp.int32)
    earlier = jnp.cumsum(onehot, axis=0) - onehot
    within = jnp.sum(earlier * onehot, axis=1)
    counts = jnp.sum(onehot.reshape(ranks, per_rank, ranks), axis=1)
    starts = jnp.cumsum(counts, axis=0) - counts
    return (within, counts, starts)


def normalize(rows, in_prefix, level_row, level_table, norm_gain):
    picks = (
        level_row[:, None] == jnp.arange(level_table.shape[0], dtype=jnp.int32)[None, :]
    ) & in_prefix[:, None]
    added = jnp.dot(picks.astype(jnp.bfloat16), level_table, preferred_element_type=jnp.float32)
    shifted = rows.astype(jnp.float32) + added
    factor = lax.rsqrt(jnp.mean(shifted * shifted, axis=-1, keepdims=True) + EPS)
    return (shifted * factor * norm_gain).astype(jnp.bfloat16)


def fold_keys(state, queries, query_clip, query_prefix, pairs, key_clip, key_prefix):
    width = queries.shape[1]
    heads_here = width // HEAD_DIM
    factor = HEAD_DIM ** (-0.5)
    allowed_query = jnp.logical_not(query_prefix)

    def absorb(carry, block):
        block_pairs, block_clip, block_prefix = block
        allowed = (query_clip[:, None] == block_clip[None, :]) & (
            allowed_query[:, None] | block_prefix[None, :]
        )
        updated = []
        for head in range(heads_here):
            top, total, summed = carry[head]
            low = head * HEAD_DIM
            q_head = queries[:, low : low + HEAD_DIM]
            k_head = block_pairs[:, low : low + HEAD_DIM]
            v_head = block_pairs[:, width + low : width + low + HEAD_DIM]
            scores = (
                lax.dot_general(
                    q_head, k_head, (((1,), (1,)), ((), ())), preferred_element_type=jnp.float32
                )
                * factor
            )
            masked = jnp.where(allowed, scores, NEG)
            new_top = jnp.maximum(top, jnp.max(masked, axis=1, keepdims=True))
            fade = jnp.exp(top - new_top)
            weights = jnp.where(allowed, jnp.exp(scores - new_top), 0.0)
            total = total * fade + jnp.sum(weights, axis=1, keepdims=True)
            summed = summed * fade + jnp.dot(
                weights.astype(jnp.bfloat16), v_head, preferred_element_type=jnp.float32
            )
            updated.append((new_top, total, summed))
        return (tuple(updated), None)

    count = pairs.shape[0]
    step = 2048 if count > 2048 and count % 2048 == 0 else count
    if step == count:
        result, unused = absorb(state, (pairs, key_clip, key_prefix))
        return result
    stacked = (
        pairs.reshape(count // step, step, pairs.shape[1]),
        key_clip.reshape(count // step, step),
        key_prefix.reshape(count // step, step),
    )
    result, unused = lax.scan(absorb, state, stacked)
    return result


def body(
    inputs,
    norm_gain,
    level_table,
    w_qkv,
    w_out,
    clip_lengths,
    prefix_lengths,
    noise_levels,
    token_rank,
):
    ranks = lax.axis_size("ctx")
    rank_here = lax.axis_index("ctx")
    per_dev = inputs.shape[0]
    slots = 2 * per_dev // ranks
    local_width = w_qkv.shape[2]
    heads_here = local_width // HEAD_DIM
    total_rows = per_dev * ranks
    clip_of, in_prefix, level_row = clip_tables(
        total_rows, clip_lengths, prefix_lengths, noise_levels
    )
    within, counts, starts = rank_tables(token_rank, ranks, per_dev)
    place = token_rank * per_dev + within
    order = (
        jnp.zeros((total_rows,), jnp.int32).at[place].set(jnp.arange(total_rows, dtype=jnp.int32))
    )
    first = rank_here * per_dev
    own_rank = lax.dynamic_slice_in_dim(token_rank, first, per_dev, 0)
    own_within = lax.dynamic_slice_in_dim(within, first, per_dev, 0)
    send_starts = lax.dynamic_slice_in_dim(starts, rank_here, 1, 0)[0]
    recv_counts = lax.dynamic_slice_in_dim(counts, rank_here, 1, 1)[:, 0]
    recv_starts = lax.dynamic_slice_in_dim(starts, rank_here, 1, 1)[:, 0]
    balanced_rows = lax.dynamic_slice_in_dim(order, first, per_dev, 0)
    target = own_rank * slots + own_within - send_starts[own_rank]
    buffer = jnp.zeros((ranks * slots, inputs.shape[1]), inputs.dtype).at[target].set(inputs)
    received = lax.all_to_all(
        buffer.reshape(ranks, slots, inputs.shape[1]),
        "ctx",
        split_axis=0,
        concat_axis=0,
        tiled=True,
    )
    spots = jnp.arange(slots, dtype=jnp.int32)[None, :]
    index = jnp.where(spots < recv_counts[:, None], recv_starts[:, None] + spots, per_dev).reshape(
        -1
    )
    flat = received.reshape(ranks * slots, received.shape[2])
    rows = jnp.zeros((per_dev, received.shape[2]), received.dtype).at[index].set(flat, mode="drop")
    full_rows = lax.all_gather(rows, "head", axis=1, tiled=True)
    normed = normalize(
        full_rows, in_prefix[balanced_rows], level_row[balanced_rows], level_table, norm_gain
    )
    qkv = jnp.dot(
        normed, w_qkv.reshape(w_qkv.shape[0], 3 * local_width), preferred_element_type=jnp.float32
    ).astype(jnp.bfloat16)
    start_state = tuple(
        (
            (
                jnp.full((per_dev, 1), NEG, jnp.float32),
                jnp.zeros((per_dev, 1), jnp.float32),
                jnp.zeros((per_dev, HEAD_DIM), jnp.float32),
            )
            for head in range(heads_here)
        )
    )
    key_clip = clip_of[order]
    key_prefix = in_prefix[order]
    query_clip = lax.dynamic_slice_in_dim(key_clip, first, per_dev, 0)
    query_prefix = lax.dynamic_slice_in_dim(key_prefix, first, per_dev, 0)
    queries = qkv[:, :local_width]
    pairs = qkv[:, local_width:]
    state = fold_keys(
        start_state,
        queries,
        query_clip,
        query_prefix,
        lax.all_gather(pairs, "ctx", axis=0, tiled=True),
        key_clip,
        key_prefix,
    )
    parts = [state[head][2] / state[head][1] for head in range(heads_here)]
    attention = jnp.concatenate(parts, axis=1).astype(jnp.bfloat16)
    terms = jnp.dot(attention, w_out, preferred_element_type=jnp.float32)
    return lax.psum_scatter(terms.astype(jnp.bfloat16), "head", scatter_dimension=1, tiled=True)


def solution(mesh):
    in_specs = (
        P("ctx", "head"),
        P(),
        P(),
        P(None, None, "head"),
        P("head", None),
        P(),
        P(),
        P(),
        P(),
    )
    out_specs = P("ctx", "head")
    return jax.shard_map(body, mesh=mesh, in_specs=in_specs, out_specs=out_specs, check_vma=False)
```

profile of v0, /device:TPU:0, one launch (start us, length us, event | category | flops | bytes accessed | tf_op | source)
XLA Modules:
  0.0 527.9 jit_solution(1887254935546727747)
XLA Ops:
  15.7 10.7 %compare_select_fusion.4 = s32[320]{0:T(512)S(1)} fusion(s32[5120]{0:T(1024)S(1)} %fusion.344, s32[]{:T(128)S(6)} %select_n.139, s32[5120]{0:T(1024)} %param.17, s32[]{:T(128)} %bitcast.4, s32[]{:T(128)} %bitcast.5, s32[]{:T(128)} %bitcast.6, s32[]{:T(128)} %bitcast.7, s32[]{:T(128)} %bitcast.8, s32[]{:T(128)} %bitcast.9, s32[]{:T(128)} %bitcast.10, ...), kind=kLoop, calls=%fused_computation.232 | loop fusion | flops 12480 | bytes 3908 | tf_op jit(solution)/shard_map/select_n | solution.py:129
  30.7 7.3 %all-to-all-start = ((bf16[16,40,1536]{2,1,0:T(8,128)(2,1)}), bf16[16,40,1536]{2,1,0:T(8,128)(2,1)S(1)}, u32[]{:S(2)}, u32[]{:S(2)}) async-start(bf16[16,40,1536]{2,1,0:T(8,128)(2,1)} %bitcast.20), calls=%async_computation | async-start | bytes 3932160 | tf_op jit(solution)/shard_map/all_to_all | solution.py:130
  38.5 38.4 %all-to-all-done = bf16[16,40,1536]{2,1,0:T(8,128)(2,1)S(1)} async-done(((bf16[16,40,1536]{2,1,0:T(8,128)(2,1)}), bf16[16,40,1536]{2,1,0:T(8,128)(2,1)S(1)}, u32[]{:S(2)}, u32[]{:S(2)}) %all-to-all-start) | async-done | bytes 1966112 | tf_op jit(solution)/shard_map/all_to_all | solution.py:130
  76.9 6.9 %scatter_custom_fusion.2 = bf16[320,1536]{1,0:T(8,128)(2,1)} fusion(s32[640]{0:T(1024)S(1)} %fusion.365, bf16[640,1536]{1,0:T(8,128)(2,1)S(1)} %bitcast.67, bf16[]{:T(256)} %constant.21.clone.1), kind=kCustom, calls=%fused_computation.185 | custom fusion | bytes 983042 | tf_op jit(solution)/shard_map/scatter | solution.py:142
  84.1 19.6 %scatter_custom_fusion = s32[5120]{0:T(1024)S(1)} fusion(s32[5120]{0:T(1024)S(1)} %compare_select_fusion.1, s32[5120]{0:T(1024)S(1)} %iota.32, s32[]{:T(128)} %constant.16.clone.1), kind=kCustom, calls=%fused_computation.225 | custom fusion | bytes 20484 | tf_op jit(solution)/shard_map/scatter | solution.py:119
  108.9 36.7 %copy.11 = bf16[3072,3,1536]{0,2,1:T(8,128)(2,1)} copy(bf16[3072,3,1536]{2,0,1:T(8,128)(2,1)} %param.12) | data formatting | bytes 56623104 | tf_op args[3]
  148.0 14.4 %convolution_convert_fusion = bf16[320,4608]{1,0:T(8,128)(2,1)S(1)} fusion(bf16[3072,4608]{0,1:T(8,128)(2,1)} %bitcast.64, f32[320,3072]{1,0:T(8,128)S(1)} %get-tuple-element.75, f32[3072]{0:T(1024)S(1)} %copy-done.10, f32[320]{0:T(512)S(1)} %add_rsqrt_fusion), kind=kOutput, calls=%fused_computation.19 | convolution fusion | flops 9064120320 | bytes 35206400 | tf_op jit(solution)/shard_map/dot_general | solution.py:147
  164.0 28.7 %gather_fusion = s32[5120]{0:T(1024)S(1)} fusion(s32[5120]{0:T(1024)S(1)} %convert_reduce_fusion.1, s32[5120]{0:T(1024)S(1)} %fusion.362), kind=kCustom, calls=%fused_computation | custom fusion | bytes 61440 | tf_op jit(solution)/shard_map/gather | solution.py:160
  192.6 32.4 %gather_fusion.1 = pred[5120]{0:T(1024)(128)(4,1)S(1)} fusion(pred[5120]{0:T(1024)(128)(4,1)S(1)} %subtract_compare_fusion, s32[5120]{0:T(1024)S(1)} %fusion.362), kind=kCustom, calls=%fused_computation.1 | custom fusion | bytes 30720 | tf_op jit(solution)/shard_map/gather | solution.py:161
  225.2 103.1 %all-gather.5.cloned.1.call-done = bf16[5120,3072]{1,0:T(8,128)(2,1)} async-done(((bf16[320,3072]{1,0:T(8,128)(2,1)}), bf16[5120,3072]{1,0:T(8,128)(2,1)}) %all-gather.5.cloned.1.call-update) | async-done | bytes 31457296 | tf_op jit(solution)/shard_map/all_gather | solution.py:171
  330.6 7.8 %select_reduce_fusion = (f32[320]{0:T(512)S(1)}, f32[320]{0:T(512)S(1)}, f32[320,5120]{1,0:T(8,128)}) fusion(pred[5120]{0:T(1024)(128)(4,1)S(1)} %gather_fusion.1, pred[320]{0:T(512)(128)(4,1)S(1)} %dynamic-slice_not_fusion, s32[5120]{0:T(1024)S(1)} %gather_fusion, s32[320]{0:T(512)S(1)} %dynamic_slice.24, f32[320,5120]{1,0:T(8,128)S(1)} %convolution_multiply_fusion.11, ...), kind=kOutput, calls=%fused_computation.21 | convolution fusion | flops 432536960 | bytes 14530560 | tf_op jit(solution)/shard_map/dot_general | solution.py:65
  338.4 5.0 convolution_multiply_fusion.1
  343.5 5.0 convolution_multiply_fusion.2
  348.5 5.0 convolution_multiply_fusion.3
  353.5 5.0 convolution_multiply_fusion.4
  358.6 5.1 convolution_multiply_fusion.5
  363.6 5.1 convolution_multiply_fusion.6
  368.7 5.1 convolution_multiply_fusion.7
  373.8 5.1 convolution_multiply_fusion.8
  378.9 5.3 convolution_multiply_fusion.9
  384.1 29.5 %fusion.22 = (f32[320]{0:T(512)S(1)}, f32[320]{0:T(512)S(1)}, f32[320]{0:T(512)S(1)}, f32[320]{0:T(512)S(1)}, f32[320]{0:T(512)S(1)}, /*index=5*/f32[320]{0:T(51...) fusion(f32[320,5120]{1,0:T(8,128)} %get-tuple-element.76, ...), kind=kOutput, calls=%fused_computation.67 | convolution fusion | flops 468578560 | bytes 80083456 | tf_op jit(solution)/shard_map/dot_general | solution.py:65
  413.8 9.5 %fusion.18 = (f32[320]{0:T(512)S(1)}, f32[320]{0:T(512)S(1)}, f32[320]{0:T(512)S(1)}) fusion(f32[320,5120]{1,0:T(8,128)} %convolution_multiply_fusion.2, f32[320]{0:T(512)S(1)} %broadcast_maximum_fusion.2, pred[5120]{0:T(1024)(128)(4,1)S(1)} %gather_fusion.1, pred[320]{0:T(512)(128)(4,1)S(1)} %dynamic-slice_not_fusion, s32[5120]{0:T(1024)S(1)} %gather_fusion, ...), kind=kLoop, calls=%fused_computation.63 | loop fusion | flops 19659840 | bytes 19695680 | tf_op jit(solution)/shard_map/reduce_sum | solution.py:74
  424.1 16.8 %fusion.20 = (f32[320]{0:T(512)S(1)}, f32[320]{0:T(512)S(1)}, f32[320]{0:T(512)S(1)}, f32[320]{0:T(512)S(1)}, f32[320]{0:T(512)S(1)}, /*index=5*/f32[320]{0:T(512)S(1)}, f32[320]{0:T(512)S(1)}) fusion(f32[320,5120]{1,0:T(8,128)} %convolution_multiply_fusion.1, f32[320]{0:T(512)S(1)} %broadcast_maximum_fusion.1, pred[5120]{0:T(1024)(128)(4,1)S(1)} %gather_fusion.1, ...), kind=kLoop, calls=%fused_computation.65 | loop fusion | flops 39319360 | bytes 45920320 | tf_op jit(solution)/shard_map/reduce_sum | solution.py:74
  490.6 30.5 %reduce-scatter.2.cloned.1.call-done = bf16[320,1536]{1,0:T(8,128)(2,1)} async-done(((bf16[320,3072]{1,0:T(8,128)(2,1)}), bf16[320,1536]{1,0:T(8,128)(2,1)}) %reduce-scatter.2.cloned.1.call-update) | async-done | bytes 983056 | tf_op jit(solution)/shard_map/reduce_scatter | solution.py:178
  (153 shorter events, 75.8 us)
Async XLA Ops:
  6.5 139.0 %copy-start = (bf16[8,3072]{1,0:T(8,128)(2,1)S(1)}, bf16[8,3072]{1,0:T(8,128)(2,1)}, u32[]{:S(2)}) copy-start(bf16[8,3072]{1,0:T(8,128)(2,1)} %param.11) | copy-start | bytes 147460
  6.5 77.5 %copy-start.6 = (s32[5120]{0:T(1024)S(1)}, s32[5120]{0:T(1024)}, u32[]{:S(2)}) copy-start(s32[5120]{0:T(1024)} %param.17) | copy-start | bytes 61444
  6.5 77.3 %copy-start.9 = (s32[8]{0:T(128)S(1)}, s32[8]{0:T(128)}, u32[]{:S(2)}) copy-start(s32[8]{0:T(128)} %param.14) | copy-start | bytes 100
  6.5 97.3 %copy-start.8 = (s32[8]{0:T(128)S(1)}, s32[8]{0:T(128)}, u32[]{:S(2)}) copy-start(s32[8]{0:T(128)} %param.15) | copy-start | bytes 100
  6.5 97.4 %copy-start.7 = (s32[8]{0:T(128)S(1)}, s32[8]{0:T(128)}, u32[]{:S(2)}) copy-start(s32[8]{0:T(128)} %param.16) | copy-start | bytes 100
  30.7 46.2 %all-to-all-start = ((bf16[16,40,1536]{2,1,0:T(8,128)(2,1)}), bf16[16,40,1536]{2,1,0:T(8,128)(2,1)S(1)}, u32[]{:S(2)}, u32[]{:S(2)}) async-start(bf16[16,40,1536]{2,1,0:T(8,128)(2,1)} %bitcast.20), calls=%async_computation | async-start | bytes 3932160 | tf_op jit(solution)/shard_map/all_to_all | solution.py:130
  38.0 107.5 %all-gather.3.cloned.1.call-start = ((), (), s32[]{:S(2)}) async-start(), calls=%async_computation.2 | async-start | bytes 2949120 | tf_op jit(solution)/shard_map/all_gather | solution.py:143
  83.8 244.5 %all-gather.5.cloned.1.call-start = ((), (), s32[]{:S(2)}) async-start(), calls=%async_computation.3 | async-start | bytes 33423360 | tf_op jit(solution)/shard_map/all_gather | solution.py:171
  108.9 39.1 %copy-start.10 = (f32[3072]{0:T(1024)S(1)}, f32[3072]{0:T(1024)}, u32[]{:S(2)}) copy-start(f32[3072]{0:T(1024)} %param.10) | copy-start | bytes 36868
  163.9 357.3 %reduce-scatter.2.cloned.1.call-start = ((), (), s32[]{:S(2)}) async-start(), calls=%async_computation.4 | async-start | bytes 2949120 | tf_op jit(solution)/shard_map/reduce_scatter | solution.py:178
  330.6 7.8 %copy-start.4 = (f32[320,5120]{1,0:T(8,128)}, f32[320,5120]{1,0:T(8,128)S(1)}, u32[]{:S(2)}) copy-start(f32[320,5120]{1,0:T(8,128)S(1)} %convolution_multiply_fusion.11) | copy-start | bytes 19660804
  413.8 9.5 %copy-start.2 = (f32[320,5120]{1,0:T(8,128)S(1)}, f32[320,5120]{1,0:T(8,128)}, u32[]{:S(2)}) copy-start(f32[320,5120]{1,0:T(8,128)} %convolution_multiply_fusion.8) | copy-start | bytes 19660804
  413.8 10.4 %copy-start.3 = (f32[320,5120]{1,0:T(8,128)S(1)}, f32[320,5120]{1,0:T(8,128)}, u32[]{:S(2)}) copy-start(f32[320,5120]{1,0:T(8,128)} %convolution_multiply_fusion.9) | copy-start | bytes 19660804
  413.8 27.3 %slice-start.14 = ((s8[6553600]{0:T(1024)(128)(4,1)}), s8[4194304]{0:T(1024)(128)(4,1)S(1)}, s32[]{:S(2)}) async-start(s8[6553600]{0:T(1024)(128)(4,1)} %bitcast.62), calls=%async_computation.19 | async-start | bytes 8388608
  424.1 16.9 %slice-start.15 = ((s8[6553600]{0:T(1024)(128)(4,1)}), s8[2359296]{0:T(1024)(128)(4,1)S(1)}, s32[]{:S(2)}) async-start(s8[6553600]{0:T(1024)(128)(4,1)} %bitcast.62), calls=%async_computation.20 | async-start | bytes 4718592
  452.0 7.4 %slice-start.4 = ((s8[6553600]{0:T(1024)(128)(4,1)}), s8[4194304]{0:T(1024)(128)(4,1)S(1)}, s32[]{:S(2)}) async-start(s8[6553600]{0:T(1024)(128)(4,1)} %bitcast.52), calls=%async_computation.9 | async-start | bytes 8388608
  455.7 7.8 %slice-start.2 = ((s8[6553600]{0:T(1024)(128)(4,1)}), s8[4194304]{0:T(1024)(128)(4,1)S(1)}, s32[]{:S(2)}) async-start(s8[6553600]{0:T(1024)(128)(4,1)} %bitcast.50), calls=%async_computation.7 | async-start | bytes 8388608
  459.4 7.8 %slice-start.12 = ((s8[6553600]{0:T(1024)(128)(4,1)}), s8[4194304]{0:T(1024)(128)(4,1)S(1)}, s32[]{:S(2)}) async-start(s8[6553600]{0:T(1024)(128)(4,1)} %bitcast.60), calls=%async_computation.17 | async-start | bytes 8388608
  467.2 7.4 %slice-start.8 = ((s8[6553600]{0:T(1024)(128)(4,1)}), s8[4194304]{0:T(1024)(128)(4,1)S(1)}, s32[]{:S(2)}) async-start(s8[6553600]{0:T(1024)(128)(4,1)} %bitcast.56), calls=%async_computation.13 | async-start | bytes 8388608
  471.0 7.4 %slice-start = ((s8[6553600]{0:T(1024)(128)(4,1)}), s8[4194304]{0:T(1024)(128)(4,1)S(1)}, s32[]{:S(2)}) async-start(s8[6553600]{0:T(1024)(128)(4,1)} %bitcast.48), calls=%async_computation.5 | async-start | bytes 8388608
  474.7 7.4 %slice-start.16 = ((s8[6553600]{0:T(1024)(128)(4,1)}), s8[2359296]{0:T(1024)(128)(4,1)S(1)}, s32[]{:S(2)}) async-start(s8[6553600]{0:T(1024)(128)(4,1)} %bitcast.65), calls=%async_computation.21 | async-start | bytes 4718592
  478.4 7.7 %slice-start.18 = ((s8[9437184]{0:T(1024)(128)(4,1)}), s8[4194304]{0:T(1024)(128)(4,1)S(1)}, s32[]{:S(2)}) async-start(s8[9437184]{0:T(1024)(128)(4,1)} %bitcast.73), calls=%async_computation.23 | async-start | bytes 8388608
  478.4 7.7 %slice-start.19 = ((s8[9437184]{0:T(1024)(128)(4,1)}), s8[4194304]{0:T(1024)(128)(4,1)S(1)}, s32[]{:S(2)}) async-start(s8[9437184]{0:T(1024)(128)(4,1)} %bitcast.73), calls=%async_computation.24 | async-start | bytes 8388608
  486.2 35.0 %copy-start.1 = (bf16[8,3072]{1,0:T(8,128)(2,1)S(1)}, bf16[8,3072]{1,0:T(8,128)(2,1)}, u32[]{:S(2)}) copy-start(bf16[8,3072]{1,0:T(8,128)(2,1)} %param.11) | copy-start | bytes 147460
  (12 other events, 52.5 us)
Sparse Core Ops, SparseCore 0:
  83.9 37.6 all-gather.2
  164.0 164.2 all-gather.4
  490.8 30.3 reduce-scatter.1
where the time goes:
time: 536 us; the launch traced here: 528 us
  waiting for transfers between devices  172 us (32%)
  matrix products  151 us (28%)
  local copies, waits for them, and re-layouts  138 us (26%)
  other arithmetic  45 us (8%)
  between operations  14.1 us (3%)
  starting transfers between devices  7.47 us (1%)
    all_gather x1, waiting for transfers between devices, body(): lax.all_gather(pairs, 'ctx', axis=0, tiled=True)  103 us
    dot_general x12, matrix products, absorb(): lax.dot_general(q_head, k_head, (((1,), (1,)), ((), ())), preferred_eleme...  85.3 us
    dot_general x12, matrix products, absorb(): jnp.dot(weights.astype(jnp.bfloat16), v_head, preferred_element_type=jnp....  44.6 us
    all_to_all x1, waiting for transfers between devices, body(): lax.all_to_all(buffer.reshape(ranks, slots, inputs.shape[1]), 'ctx', spli...  38.4 us
    unnamed x65, local copies, waits for them, and re-layouts  37.7 us
    gather x1, local copies, waits for them, and re-layouts, body(): key_prefix = in_prefix[order]  32.4 us
    reduce_scatter x1, waiting for transfers between devices, body(): lax.psum_scatter(terms.astype(jnp.bfloat16), 'head', scatter_dimension=1,...  30.5 us
    gather x1, local copies, waits for them, and re-layouts, body(): key_clip = clip_of[order]  28.7 us
  transfers between devices with their start and end apart: 4, of which 3 were waited for; matrix products, arithmetic and copies ran while one was open for 23% of the time, Pallas kernels for 0%

commit v1 on v0

--- a/solution.py
+++ b/solution.py
@@ -1,6 +1,8 @@
 import jax
 import jax.numpy as jnp
 from jax import lax
+from jax.experimental import pallas as pl
+from jax.experimental.pallas import tpu as pltpu
 from jax.sharding import PartitionSpec as P
 
 HEAD_DIM = 128
@@ -8,6 +10,9 @@
 
 NEG = -1e30
 EPS = 1e-06
+MAXCLIP = 2560
+LOG2E = 1.4426950408889634
+VMEM_LIMIT = 48 * 1024 * 1024
 
 
 def clip_tables(total_rows, clip_lengths, prefix_lengths, noise_levels):
@@ -92,7 +97,7 @@
     return result
 
 
-def body(
+def gathered_body(
     inputs,
     norm_gain,
     level_table,
@@ -178,6 +183,297 @@
     return lax.psum_scatter(terms.astype(jnp.bfloat16), "head", scatter_dimension=1, tiled=True)
 
 
+def project_kernel(spot_ref, rows_ref, w_ref, out_ref):
+    weights = jnp.concatenate([w_ref[0], w_ref[1], w_ref[2]], axis=1)
+    out_ref[0] = jnp.dot(
+        rows_ref[...], weights, preferred_element_type=jnp.float32
+    ).astype(jnp.bfloat16)
+
+
+def project_heads(normed, w_parts, spot, first_head, count, group_heads):
+    rows, depth = normed.shape
+    return pl.pallas_call(
+        project_kernel,
+        grid_spec=pltpu.PrefetchScalarGridSpec(
+            num_scalar_prefetch=1,
+            grid=(4, count),
+            in_specs=[
+                pl.BlockSpec((rows, depth), lambda d, h, spot_ref: (0, 0)),
+                pl.BlockSpec(
+                    (3, depth, HEAD_DIM),
+                    lambda d, h, spot_ref: (
+                        0,
+                        0,
+                        group_heads * jnp.bitwise_xor(spot_ref[0], d) + first_head + h,
+                    ),
+                ),
+            ],
+            out_specs=pl.BlockSpec((1, rows, 3 * HEAD_DIM), lambda d, h, spot_ref: (d, 0, h)),
+        ),
+        out_shape=jax.ShapeDtypeStruct((4, rows, count * 3 * HEAD_DIM), jnp.bfloat16),
+        compiler_params=pltpu.CompilerParams(vmem_limit_bytes=VMEM_LIMIT),
+        cost_estimate=pl.CostEstimate(
+            flops=2 * rows * depth * 12 * HEAD_DIM * count,
+            bytes_accessed=2 * depth * 12 * HEAD_DIM * count,
+            transcendentals=0,
+        ),
+    )(spot, normed, w_parts)
+
+
+def attend_kernel(*refs):
+    blocks = refs[:8]
+    key_code_ref, low_ref, high_ref, out_ref, q_all, k_all, v_all = refs[8:]
+    rows = blocks[0].shape[-2]
+    tile = out_ref.shape[0]
+    step = pl.program_id(1)
+
+    @pl.when(step == 0)
+    def _():
+        for index, block in enumerate(blocks):
+            spot = slice(index * rows, (index + 1) * rows)
+            lead = (0,) if len(block.shape) == 3 else ()
+            if index < 4:
+                q_all[spot, :] = block[lead + (slice(None), slice(0, HEAD_DIM))]
+            k_all[spot, :] = block[lead + (slice(None), slice(HEAD_DIM, 2 * HEAD_DIM))]
+            v_all[spot, :] = block[lead + (slice(None), slice(2 * HEAD_DIM, 3 * HEAD_DIM))]
+
+    queries = q_all[pl.ds(pl.multiple_of(step * tile, tile), tile), :]
+    scores = lax.dot_general(
+        queries, k_all[...], (((1,), (1,)), ((), ())), preferred_element_type=jnp.float32
+    )
+    code = key_code_ref[...]
+    allowed = (code >= low_ref[...]) & (code <= high_ref[...])
+    masked = jnp.where(allowed, scores, NEG)
+    top = jnp.max(masked, axis=1, keepdims=True)
+    weights = jnp.exp2((masked - top) * (HEAD_DIM ** (-0.5) * LOG2E))
+    total = jnp.sum(weights, axis=1, keepdims=True)
+    summed = jnp.dot(weights.astype(jnp.bfloat16), v_all[...], preferred_element_type=jnp.float32)
+    out_ref[...] = (summed / total).astype(jnp.bfloat16)
+
+
+def attend(own, others, key_code, low, high, count):
+    rows = own.shape[1]
+    keys, queries, tile = 8 * rows, 4 * rows, 256
+    width = 3 * HEAD_DIM
+    block = pl.BlockSpec((rows, width), lambda h, t: (0, h))
+    column = pl.BlockSpec((tile, 1), lambda h, t: (t, 0))
+    return pl.pallas_call(
+        attend_kernel,
+        grid=(count, queries // tile),
+        in_specs=[pl.BlockSpec((1, rows, width), lambda h, t: (0, 0, h))]
+        + [block] * 7
+        + [pl.BlockSpec((1, keys), lambda h, t: (0, 0)), column, column],
+        out_specs=pl.BlockSpec((tile, HEAD_DIM), lambda h, t: (t, h)),
+        out_shape=jax.ShapeDtypeStruct((queries, count * HEAD_DIM), jnp.bfloat16),
+        scratch_shapes=[
+            pltpu.VMEM((queries, HEAD_DIM), jnp.bfloat16),
+            pltpu.VMEM((keys, HEAD_DIM), jnp.bfloat16),
+            pltpu.VMEM((keys, HEAD_DIM), jnp.bfloat16),
+        ],
+        compiler_params=pltpu.CompilerParams(vmem_limit_bytes=VMEM_LIMIT),
+        cost_estimate=pl.CostEstimate(
+            flops=8 * queries * keys * HEAD_DIM * count,
+            bytes_accessed=8 * rows * width * 2 * count,
+            transcendentals=queries * keys * count,
+        ),
+    )(own, *others, key_code, low, high)
+
+
+def place_kernel(base_ref, own_ref, other_ref, place_ref, out_ref):
+    rows = out_ref.shape[1]
+    half = own_ref.shape[0]
+    wanted = base_ref[pl.program_id(0)] + lax.broadcasted_iota(jnp.int32, (rows, 1), 0)
+    picks = jnp.where(place_ref[...] == wanted, 1.0, 0.0).astype(jnp.bfloat16)
+    out_ref[0] = (
+        jnp.dot(picks[:, :half], own_ref[...], preferred_element_type=jnp.float32)
+        + jnp.dot(picks[:, half:], other_ref[...], preferred_element_type=jnp.float32)
+    ).astype(jnp.bfloat16)
+
+
+def place_rows(bases, own, other, places, rows):
+    slots = bases.shape[0]
+    half, width = own.shape
+    return pl.pallas_call(
+        place_kernel,
+        grid_spec=pltpu.PrefetchScalarGridSpec(
+            num_scalar_prefetch=1,
+            grid=(slots,),
+            in_specs=[
+                pl.BlockSpec((half, width), lambda d, base_ref: (0, 0)),
+                pl.BlockSpec((half, width), lambda d, base_ref: (0, 0)),
+                pl.BlockSpec((1, 2 * half), lambda d, base_ref: (0, 0)),
+            ],
+            out_specs=pl.BlockSpec((1, rows, width), lambda d, base_ref: (d, 0, 0)),
+        ),
+        out_shape=jax.ShapeDtypeStruct((slots, rows, width), jnp.bfloat16),
+        compiler_params=pltpu.CompilerParams(vmem_limit_bytes=VMEM_LIMIT),
+        cost_estimate=pl.CostEstimate(
+            flops=4 * slots * rows * half * width,
+            bytes_accessed=4 * half * width,
+            transcendentals=0,
+        ),
+    )(bases, own, other, places)
+
+
+def out_kernel(spot_ref, *refs):
+    out_ref = refs[-1]
+    pieces = (len(refs) - 5) // 4
+    total = None
+    for d in range(4):
+        rows = jnp.concatenate([ref[...] for ref in refs[d * pieces : (d + 1) * pieces]], axis=1)
+        term = jnp.dot(rows, refs[4 * pieces + d][...], preferred_element_type=jnp.float32)
+        total = term if total is None else total + term
+    out_ref[...] = total.astype(out_ref.dtype)
+
+
+def project_out(attention, w_out, spot, side, dtype):
+    rows = attention[0][0].shape[0]
+    group = w_out.shape[0] // 4
+    columns, tile = w_out.shape[1] // 2, 512
+    tiles = columns // tile
+    pieces = [piece for slot in attention for piece in slot]
+
+    def w_spec(d):
+        return pl.BlockSpec(
+            (group, tile),
+            lambda t, spot_ref: (jnp.bitwise_xor(spot_ref[0], d), spot_ref[1] * tiles + t),
+        )
+
+    return pl.pallas_call(
+        out_kernel,
+        grid_spec=pltpu.PrefetchScalarGridSpec(
+            num_scalar_prefetch=1,
+            grid=(tiles,),
+            in_specs=[pl.BlockSpec(piece.shape, lambda t, spot_ref: (0, 0)) for piece in pieces]
+            + [w_spec(d) for d in range(4)],
+            out_specs=pl.BlockSpec((rows, tile), lambda t, spot_ref: (0, t)),
+        ),
+        out_shape=jax.ShapeDtypeStruct((rows, columns), dtype),
+        compiler_params=pltpu.CompilerParams(vmem_limit_bytes=VMEM_LIMIT),
+        cost_estimate=pl.CostEstimate(
+            flops=2 * rows * columns * 4 * group,
+            bytes_accessed=2 * columns * 4 * group,
+            transcendentals=0,
+        ),
+    )(jnp.stack([spot, side]), *pieces, *([w_out] * 4))
+
+
+def row_facts(rows, clip_lengths, prefix_lengths, noise_levels):
+    ends = jnp.cumsum(clip_lengths)
+    begins = ends - clip_lengths
+    lead = begins + jnp.minimum(prefix_lengths, clip_lengths)
+    past = rows[:, None] >= ends[None, :]
+    clip = jnp.sum(past.astype(jnp.int32), axis=1)
+    inside = (rows[:, None] >= begins[None, :]) & jnp.logical_not(past)
+    in_prefix = jnp.any(inside & (rows[:, None] < lead[None, :]), axis=1)
+    level = jnp.sum(jnp.where(inside, noise_levels[None, :], 0), axis=1)
+    return clip, in_prefix, level
+
+
+CHUNKS = ((0, 1), (1, 1), (2, 1))
+
+
+def halved_body(
+    inputs,
+    norm_gain,
+    level_table,
+    w_qkv,
+    w_out,
+    clip_lengths,
+    prefix_lengths,
+    noise_levels,
+    token_rank,
+):
+    rank_here = lax.axis_index("ctx")
+    side = lax.axis_index("head")
+    per_dev = inputs.shape[0]
+    ranks = 16
+    half_rows = 8 * per_dev
+    local_width = w_qkv.shape[2]
+    group_heads = local_width // HEAD_DIM // 4
+    half, block = rank_here // 8, rank_here % 8
+    spot = block // 2
+
+    def exchange(array, flip, only=None):
+        pairs = [(r, r ^ flip) for r in range(ranks) if only is None or only(r)]
+        return lax.ppermute(array, "ctx", pairs)
+
+    begins = jnp.cumsum(clip_lengths) - clip_lengths
+    start = jnp.sum(jnp.where(clip_lengths == MAXCLIP, begins, 0))
+    early = start <= half_rows // 2
+
+    def packed_row(spots):
+        swapped = jnp.where(early, spots < start, spots >= start)
+        return spots + half_rows * (half ^ swapped.astype(jnp.int32)), swapped
+
+    own_packed, own_swapped = packed_row(block * per_dev + jnp.arange(per_dev, dtype=jnp.int32))
+    moved = lax.cond(
+        early,
+        lambda x: exchange(x, 8, lambda r: r % 8 < 4),
+        lambda x: exchange(x, 8, lambda r: r % 8 >= 4),
+        inputs,
+    )
+    rows = jnp.where(own_swapped[:, None], moved, inputs)
+    other = lax.ppermute(rows, "head", [(0, 1), (1, 0)])
+    full_rows = jnp.where(
+        side == 0,
+        jnp.concatenate([rows, other], axis=1),
+        jnp.concatenate([other, rows], axis=1),
+    )
+    unused, own_prefix, own_level = row_facts(
+        own_packed, clip_lengths, prefix_lengths, noise_levels
+    )
+    normed = normalize(full_rows, own_prefix, own_level, level_table, norm_gain)
+
+    flips = jnp.array([0, 2, 4, 6, 1, 3, 5, 7], jnp.int32)
+    order = block ^ flips
+    spots = (order[:, None] * per_dev + jnp.arange(per_dev, dtype=jnp.int32)[None, :]).reshape(-1)
+    packed, swapped = packed_row(spots)
+    clip, in_prefix, unused = row_facts(packed, clip_lengths, prefix_lengths, noise_levels)
+    code = 2 * clip + jnp.where(in_prefix, 0, 1)
+    key_code = code.reshape(1, half_rows)
+    high = code[: half_rows // 2].reshape(-1, 1)
+    low = (2 * clip[: half_rows // 2]).reshape(-1, 1)
+
+    within, unused, unused = rank_tables(token_rank, ranks, per_dev)
+    place = token_rank * per_dev + within
+    every_spot = jnp.arange(half_rows, dtype=jnp.int32)
+    every_packed, unused = packed_row(every_spot)
+    half_place = jnp.where(every_packed >= half_rows, place[half_rows:], place[:half_rows])
+    half_place = half_place.reshape(8, per_dev)
+    places = jnp.sum(
+        jnp.where(
+            (order[:, None] == jnp.arange(8, dtype=jnp.int32)[None, :])[:, :, None],
+            half_place[None],
+            0,
+        ),
+        axis=1,
+    ).reshape(1, half_rows)
+    bases = per_dev * (rank_here ^ (2 * jnp.arange(8, dtype=jnp.int32)))
+
+    w_parts = jnp.transpose(w_qkv, (1, 0, 2))
+    spot_array = spot.reshape(1)
+    attention = [[], [], [], []]
+    for first_head, count in CHUNKS:
+        mine = project_heads(normed, w_parts, spot_array, first_head, count, group_heads)
+        blocks = [mine[0]] + [exchange(mine[d], 2 * d) for d in range(1, 4)]
+        pairs = [exchange(part, 1) for part in blocks]
+        result = attend(mine, blocks[1:] + pairs, key_code, low, high, count)
+        paired = exchange(result, 1)
+        across = place_rows(bases[4:], result, paired, places, per_dev)
+        arrived = exchange(across, 8)
+        staying = place_rows(bases[:4], result, paired, places, per_dev)
+        joined = staying + arrived
+        attention[0].append(joined[0])
+        for d in range(1, 4):
+            attention[d].append(exchange(joined[d], 2 * d))
+
+    away = project_out(attention, w_out, spot, 1 - side, jnp.bfloat16)
+    away = lax.ppermute(away, "head", [(0, 1), (1, 0)])
+    stay = project_out(attention, w_out, spot, side, jnp.float32)
+    return (stay + away.astype(jnp.float32)).astype(jnp.bfloat16)
+
+
 def solution(mesh):
     in_specs = (
         P("ctx", "head"),
@@ -191,4 +487,17 @@
         P(),
     )
     out_specs = P("ctx", "head")
+
+    def body(inputs, norm_gain, level_table, w_qkv, *rest):
+        ranks, sides = mesh.shape["ctx"], mesh.shape["head"]
+        heads_here = w_qkv.shape[2] // HEAD_DIM
+        halved = (
+            ranks == 16
+            and sides == 2
+            and ranks * inputs.shape[0] == 2 * MAXCLIP
+            and heads_here % 4 == 0
+        )
+        run = halved_body if halved else gathered_body
+        return run(inputs, norm_gain, level_table, w_qkv, *rest)
+
     return jax.shard_map(body, mesh=mesh, in_specs=in_specs, out_specs=out_specs, check_vma=False)

time: 536 us -> 226 us (0.42); the launches traced: 528 us -> 225 us
  matrix products: 151 us -> 1.04 us
  local copies, waits for them, and re-layouts: 138 us -> 9.51 us
  waiting for transfers between devices: 172 us -> 84.9 us
  Pallas kernels: 0 us -> 74.6 us
  starting transfers between devices: 7.47 us -> 38.5 us
  other arithmetic: 45 us -> 15.7 us
  between operations: 14.1 us -> 1.1 us
    dot_general x26 -> x0, matrix products: 149 us -> none  [the longest x12 85.3 us: absorb(): lax.dot_general(q_head, k_head, (((1,), (1,)), ((), ())), preferred_eleme...]
    all_gather x2 -> x0, waiting for transfers between devices: 103 us -> none  [the longest x1 103 us: body(): lax.all_gather(pairs, 'ctx', axis=0, tiled=True)]
    ppermute x0 -> x39, waiting for transfers between devices: none -> 84.9 us  [the longest x37 56.2 us: exchange(): return lax.ppermute(array, 'ctx', pairs)]
    pallas_call x0 -> x14, Pallas kernels: none -> 74.6 us  [the longest x3 25.8 us: attend(): pl.pallas_call(attend_kernel, grid=(count, queries // tile), in_specs=[pl...]
    gather x5 -> x0, local copies, waits for them, and re-layouts: 66.5 us -> none  [the longest x1 32.4 us: body(): key_prefix = in_prefix[order]]
    ppermute x0 -> x39, starting transfers between devices: none -> 38.5 us  [the longest x37 35.6 us: exchange(): return lax.ppermute(array, 'ctx', pairs)]
    all_to_all x1 -> x0, waiting for transfers between devices: 38.4 us -> none  [body(): lax.all_to_all(buffer.reshape(ranks, slots, inputs.shape[1]), 'ctx', spli...]
    unnamed x65 -> x26, local copies, waits for them, and re-layouts: 37.7 us -> 4.49 us
  transfers between devices with their start and end apart: 4 -> 39, of which waited for: 3 -> 13; matrix products, arithmetic and copies ran while one was open for 23% -> 6% of each run, Pallas kernels for 0% -> 25%
where the time goes in v1:
time: 226 us; the launch traced here: 225 us
  waiting for transfers between devices  84.9 us (38%)
  Pallas kernels  74.6 us (33%)
  starting transfers between devices  38.5 us (17%)
  other arithmetic  15.7 us (7%)
  local copies, waits for them, and re-layouts  9.51 us (4%)
    ppermute x37, waiting for transfers between devices, exchange(): return lax.ppermute(array, 'ctx', pairs)  56.2 us
    ppermute x37, starting transfers between devices, exchange(): return lax.ppermute(array, 'ctx', pairs)  35.6 us
    pallas_call x3, Pallas kernels, attend(): pl.pallas_call(attend_kernel, grid=(count, queries // tile), in_specs=[pl...  25.8 us
    pallas_call x3, Pallas kernels, project_heads(): pl.pallas_call(project_kernel, grid_spec=pltpu.PrefetchScalarGridSpec(num...  21.1 us
    pallas_call x6, Pallas kernels, place_rows(): pl.pallas_call(place_kernel, grid_spec=pltpu.PrefetchScalarGridSpec(num_s...  17.5 us
    ppermute x1, waiting for transfers between devices, halved_body(): away = lax.ppermute(away, 'head', [(0, 1), (1, 0)])  16.5 us
    ppermute x1, waiting for transfers between devices, halved_body(): other = lax.ppermute(rows, 'head', [(0, 1), (1, 0)])  12.2 us
    pallas_call x2, Pallas kernels, project_out(): pl.pallas_call(out_kernel, grid_spec=pltpu.PrefetchScalarGridSpec(num_sca...  10.1 us
  transfers between devices with their start and end apart: 39, of which 13 were waited for; matrix products, arithmetic and copies ran while one was open for 6% of the time, Pallas kernels for 25%

profile of v1, /device:TPU:0, one launch (start us, length us, event | category | flops | bytes accessed | tf_op | source)
XLA Modules:
  0.0 225.4 jit_solution(11335559105931549107)
XLA Ops:
  3.5 28.0 %conditional.1 = (bf16[320,1536]{1,0:T(8,128)(2,1)}) conditional(s32[]{:T(128)} %convert_element_type.45, bf16[320,1536]{1,0:T(8,128)(2,1)} %param.12, bf16[320,1536]{1,0:T(8,128)(2,1)} %param.12), branch_computations={%region_2.3_spmd, %region_3.4_spmd} | conditional | bytes 3932208 | solution.py:410
  3.5 6.0 %collective-permute-start.1 = (bf16[320,1536]{1,0:T(8,128)(2,1)}, bf16[320,1536]{1,0:T(8,128)(2,1)}, u32[]{:S(2)}, u32[]{:S(2)}) collective-permute-start(bf16[320,1536]{1,0:T(8,128)(2,1)} %param.1), channel_id=1, source_target_pairs={{0,16},{2,18},{4,20},{6,22},{16,0},{18,2},{20,4},{22,6},{1,17},{3,... | collective-permute-start | bytes 2949128 | tf_op jit(solution)/shard_map/cond/branch_1_fun/ppermute | solution.py:399
  9.5 22.1 %collective-permute-done.1 = bf16[320,1536]{1,0:T(8,128)(2,1)} collective-permute-done((bf16[320,1536]{1,0:T(8,128)(2,1)}, bf16[320,1536]{1,0:T(8,128)(2,1)}, u32[]{:S(2)}, u32[]{:S(2)}) %collective-permute-start.1) | collective-permute-done | bytes 983072 | tf_op jit(solution)/shard_map/cond/branch_1_fun/ppermute | solution.py:399
  37.1 4.7 %reduce-window.19 = s32[16,40,128]{2,1,0:T(8,128)S(1)} reduce-window(s32[16,40,128]{2,1,0:T(8,128)S(1)} %fusion.3, s32[]{:T(128)} %constant.69.clone.1), window={size=1x1x128 pad=0_0x0_0x127_0}, to_apply=%region_9.10 | reduce-window | flops 10403840 | bytes 655364 | tf_op jit(solution)/shard_map/reduce-window.1
  44.0 12.2 %collective-permute-done.2 = bf16[320,1536]{1,0:T(8,128)(2,1)S(1)} collective-permute-done((bf16[320,1536]{1,0:T(8,128)(2,1)S(1)}, bf16[320,1536]{1,0:T(8,128)(2,1)S(1)}, u32[]{:S(2)}, u32[]{:S(2)}) %collective-permute-start.2) | collective-permute-done | bytes 983072 | tf_op jit(solution)/shard_map/ppermute | solution.py:417
  58.3 7.1 %shard_map.114.refs_0_ = bf16[4,320,384]{2,1,0:T(8,128)(2,1)S(1)} custom-call(s32[1]{0:T(128)} %bitcast.spot_ref, bf16[320,3072]{1,0:T(8,128)(2,1)S(1)} %multiply_convert_fusion.rows_ref, bf16[3,3072,1536]{2,1,0:T(8,128)(2,1)} %bitcast.79), custom_call_target="tpu_custom_call" | custom-call | flops 3019898880 | bytes 9437184 | tf_op jit(solution)/shard_map/pallas_call | solution.py:195
  65.4 7.1 %shard_map.110.refs_0_ = bf16[4,320,384]{2,1,0:T(8,128)(2,1)S(1)} custom-call(s32[1]{0:T(128)} %bitcast.spot_ref, bf16[320,3072]{1,0:T(8,128)(2,1)S(1)} %multiply_convert_fusion.rows_ref, bf16[3,3072,1536]{2,1,0:T(8,128)(2,1)} %bitcast.80), custom_call_target="tpu_custom_call" | custom-call | flops 3019898880 | bytes 9437184 | tf_op jit(solution)/shard_map/pallas_call | solution.py:195
  78.1 7.0 %shard_map.106.refs_0_ = bf16[4,320,384]{2,1,0:T(8,128)(2,1)S(1)} custom-call(s32[1]{0:T(128)} %bitcast.spot_ref, bf16[320,3072]{1,0:T(8,128)(2,1)S(1)} %multiply_convert_fusion.rows_ref, bf16[3,3072,1536]{2,1,0:T(8,128)(2,1)} %bitcast.81), custom_call_target="tpu_custom_call" | custom-call | flops 3019898880 | bytes 9437184 | tf_op jit(solution)/shard_map/pallas_call | solution.py:195
  90.7 3.3 %collective-permute-done.13.refs_2_ = bf16[320,384]{1,0:T(8,128)(2,1)S(1)} collective-permute-done((bf16[320,384]{1,0:T(8,128)(2,1)S(1)}, bf16[320,384]{1,0:T(8,128)(2,1)S(1)}, u32[]{:S(2)}, u32[]{:S(2)}) %collective-permute-start.13) | collective-permute-done | bytes 245792 | tf_op jit(solution)/shard_map/ppermute | solution.py:399
  94.0 4.9 %collective-permute-done.14.refs_3_ = bf16[320,384]{1,0:T(8,128)(2,1)S(1)} collective-permute-done((bf16[320,384]{1,0:T(8,128)(2,1)S(1)}, bf16[320,384]{1,0:T(8,128)(2,1)S(1)}, u32[]{:S(2)}, u32[]{:S(2)}) %collective-permute-start.14) | collective-permute-done | bytes 245792 | tf_op jit(solution)/shard_map/ppermute | solution.py:399
  108.5 8.9 %shard_map.115.own_ref = bf16[1280,128]{1,0:T(8,128)(2,1)S(1)} custom-call(bf16[4,320,384]{2,1,0:T(8,128)(2,1)S(1)} %shard_map.114.refs_0_, bf16[320,384]{1,0:T(8,128)(2,1)} %collective-permute-done.21.refs_1_, bf16[320,384]{1,0:T(8,128)(2,1)} %collective-permute-done.22.refs_2_, bf16[320,384]{1,0:T(8,128)(2,1)} %collective-permute-done.23.refs_3_, ...), custom_call_target="tpu_custom_call" | custom-call | flops 3355443200 | bytes 1966080 | tf_op jit(solution)/shard_map/pallas_call | solution.py:260
  119.0 8.3 %shard_map.111.own_ref = bf16[1280,128]{1,0:T(8,128)(2,1)S(1)} custom-call(bf16[4,320,384]{2,1,0:T(8,128)(2,1)S(1)} %shard_map.110.refs_0_, bf16[320,384]{1,0:T(8,128)(2,1)S(1)} %collective-permute-done.12.refs_1_, bf16[320,384]{1,0:T(8,128)(2,1)S(1)} %collective-permute-done.13.refs_2_, bf16[320,384]{1,0:T(8,128)(2,1)S(1)} %copy-done.6, ...), custom_call_target="tpu_custom_call" | custom-call | flops 3355443200 | bytes 1966080 | tf_op jit(solution)/shard_map/pallas_call | solution.py:260
  127.6 8.5 %shard_map.107.own_ref = bf16[1280,128]{1,0:T(8,128)(2,1)S(1)} custom-call(bf16[4,320,384]{2,1,0:T(8,128)(2,1)S(1)} %shard_map.106.refs_0_, bf16[320,384]{1,0:T(8,128)(2,1)} %collective-permute-done.3.refs_1_, bf16[320,384]{1,0:T(8,128)(2,1)S(1)} %collective-permute-done.4.refs_2_, bf16[320,384]{1,0:T(8,128)(2,1)S(1)} %collective-permute-done.5.refs_3_, ...), custom_call_target="tpu_custom_call" | custom-call | flops 3355443200 | bytes 1966080 | tf_op jit(solution)/shard_map/pallas_call | solution.py:260
  142.3 2.9 %shard_map.113 = bf16[4,320,128]{2,1,0:T(8,128)(2,1)S(1)} custom-call(s32[4]{0:T(128)S(1)} %get-tuple-element.41.base_ref, bf16[1280,128]{1,0:T(8,128)(2,1)S(1)} %shard_map.111.own_ref, bf16[1280,128]{1,0:T(8,128)(2,1)S(1)} %collective-permute-done.19.other_ref, s32[1,2560]{1,0:T(1,128)S(1)} %reshape.183.place_ref), custom_call_target="tpu_custom_call" | custom-call | flops 838860800 | bytes 655360 | tf_op jit(solution)/shard_map/pallas_call | solution.py:296
  145.6 2.9 %shard_map.109 = bf16[4,320,128]{2,1,0:T(8,128)(2,1)S(1)} custom-call(s32[4]{0:T(128)S(1)} %get-tuple-element.41.base_ref, bf16[1280,128]{1,0:T(8,128)(2,1)S(1)} %shard_map.107.own_ref, bf16[1280,128]{1,0:T(8,128)(2,1)S(1)} %collective-permute-done.10.other_ref, s32[1,2560]{1,0:T(1,128)S(1)} %reshape.183.place_ref), custom_call_target="tpu_custom_call" | custom-call | flops 838860800 | bytes 655360 | tf_op jit(solution)/shard_map/pallas_call | solution.py:296
  151.2 2.9 %shard_map.116 = bf16[4,320,128]{2,1,0:T(8,128)(2,1)S(1)} custom-call(s32[4]{0:T(128)S(1)} %get-tuple-element.42.base_ref, bf16[1280,128]{1,0:T(8,128)(2,1)S(1)} %shard_map.115.own_ref, bf16[1280,128]{1,0:T(8,128)(2,1)S(1)} %collective-permute-done.28.other_ref, s32[1,2560]{1,0:T(1,128)S(1)} %reshape.183.place_ref), custom_call_target="tpu_custom_call" | custom-call | flops 838860800 | bytes 655360 | tf_op jit(solution)/shard_map/pallas_call | solution.py:296
  154.1 2.9 %shard_map.112 = bf16[4,320,128]{2,1,0:T(8,128)(2,1)S(1)} custom-call(s32[4]{0:T(128)S(1)} %get-tuple-element.42.base_ref, bf16[1280,128]{1,0:T(8,128)(2,1)S(1)} %shard_map.111.own_ref, bf16[1280,128]{1,0:T(8,128)(2,1)S(1)} %collective-permute-done.19.other_ref, s32[1,2560]{1,0:T(1,128)S(1)} %reshape.183.place_ref), custom_call_target="tpu_custom_call" | custom-call | flops 838860800 | bytes 655360 | tf_op jit(solution)/shard_map/pallas_call | solution.py:296
  157.0 2.9 %shard_map.108 = bf16[4,320,128]{2,1,0:T(8,128)(2,1)S(1)} custom-call(s32[4]{0:T(128)S(1)} %get-tuple-element.42.base_ref, bf16[1280,128]{1,0:T(8,128)(2,1)S(1)} %shard_map.107.own_ref, bf16[1280,128]{1,0:T(8,128)(2,1)S(1)} %collective-permute-done.10.other_ref, s32[1,2560]{1,0:T(1,128)S(1)} %reshape.183.place_ref), custom_call_target="tpu_custom_call" | custom-call | flops 838860800 | bytes 655360 | tf_op jit(solution)/shard_map/pallas_call | solution.py:296
  160.0 12.0 %collective-permute-done.29 = bf16[4,320,128]{2,1,0:T(8,128)(2,1)S(1)} collective-permute-done((bf16[4,320,128]{2,1,0:T(8,128)(2,1)S(1)}, bf16[4,320,128]{2,1,0:T(8,128)(2,1)S(1)}, u32[]{:S(2)}, u32[]{:S(2)}) %collective-permute-start.29) | collective-permute-done | bytes 327712 | tf_op jit(solution)/shard_map/ppermute | solution.py:399
  175.6 3.4 %collective-permute-done.20 = bf16[4,320,128]{2,1,0:T(8,128)(2,1)S(1)} collective-permute-done((bf16[4,320,128]{2,1,0:T(8,128)(2,1)S(1)}, bf16[4,320,128]{2,1,0:T(8,128)(2,1)S(1)}, u32[]{:S(2)}, u32[]{:S(2)}) %collective-permute-start.20) | collective-permute-done | bytes 327712 | tf_op jit(solution)/shard_map/ppermute | solution.py:399
  180.1 5.4 %collective-permute-done.11 = bf16[4,320,128]{2,1,0:T(8,128)(2,1)S(1)} collective-permute-done((bf16[4,320,128]{2,1,0:T(8,128)(2,1)S(1)}, bf16[4,320,128]{2,1,0:T(8,128)(2,1)S(1)}, u32[]{:S(2)}, u32[]{:S(2)}) %collective-permute-start.11) | collective-permute-done | bytes 327712 | tf_op jit(solution)/shard_map/ppermute | solution.py:399
  196.1 5.0 %shard_map.119 = bf16[320,1536]{1,0:T(8,128)(2,1)S(1)} custom-call(s32[2]{0:T(128)S(1)} %pad_add_fusion.1.spot_ref, bf16[320,128]{1,0:T(8,128)(2,1)S(1)} %get-tuple-element.35.refs_0_, bf16[320,128]{1,0:T(8,128)(2,1)S(1)} %get-tuple-element.31.refs_1_, bf16[320,128]{1,0:T(8,128)(2,1)S(1)} %get-tuple-element.27.refs_2_, ...), custom_call_target="tpu_custom_call" | custom-call | flops 1509949440 | bytes 4718592 | tf_op jit(solution)/shard_map/pallas_call | solution.py:342
  202.6 5.1 %shard_map.118 = f32[320,1536]{1,0:T(8,128)S(1)} custom-call(s32[2]{0:T(128)S(1)} %pad_add_fusion.spot_ref, bf16[320,128]{1,0:T(8,128)(2,1)S(1)} %get-tuple-element.35.refs_0_, bf16[320,128]{1,0:T(8,128)(2,1)S(1)} %get-tuple-element.31.refs_1_, bf16[320,128]{1,0:T(8,128)(2,1)S(1)} %get-tuple-element.27.refs_2_, ...), custom_call_target="tpu_custom_call" | custom-call | flops 1509949440 | bytes 4718592 | tf_op jit(solution)/shard_map/pallas_call | solution.py:342
  207.7 16.5 %collective-permute-done.39 = bf16[320,1536]{1,0:T(8,128)(2,1)S(1)} collective-permute-done((bf16[320,1536]{1,0:T(8,128)(2,1)S(1)}, bf16[320,1536]{1,0:T(8,128)(2,1)S(1)}, u32[]{:S(2)}, u32[]{:S(2)}) %collective-permute-start.39) | collective-permute-done | bytes 983072 | tf_op jit(solution)/shard_map/ppermute | solution.py:472
  (144 shorter events, 62.1 us)
Async XLA Ops:
  3.5 28.0 %collective-permute-start.1 = (bf16[320,1536]{1,0:T(8,128)(2,1)}, bf16[320,1536]{1,0:T(8,128)(2,1)}, u32[]{:S(2)}, u32[]{:S(2)}) collective-permute-start(bf16[320,1536]{1,0:T(8,128)(2,1)} %param.1), channel_id=1, source_target_pairs={{0,16},{2,18},{4,20},{6,22},{16,0},{18,2},{20,4},{22,6},{1,17},{3,... | collective-permute-start | bytes 2949128 | tf_op jit(solution)/shard_map/cond/branch_1_fun/ppermute | solution.py:399
  33.2 23.0 %collective-permute-start.2 = (bf16[320,1536]{1,0:T(8,128)(2,1)S(1)}, bf16[320,1536]{1,0:T(8,128)(2,1)S(1)}, u32[]{:S(2)}, u32[]{:S(2)}) collective-permute-start(bf16[320,1536]{1,0:T(8,128)(2,1)S(1)} %broadcast_select_fusion), channel_id=1, source_target_pairs={{0,1},{1,0},{2,3},{3,2},{4,5},{5,4},{6,7},{7,6},{8,9},{9,8},{10,11... | collective-permute-start | bytes 2949128 | tf_op jit(solution)/shard_map/ppermute | solution.py:417
  72.6 12.6 %collective-permute-start.21 = (bf16[320,384]{1,0:T(8,128)(2,1)S(1)}, bf16[320,384]{1,0:T(8,128)(2,1)}, u32[]{:S(2)}, u32[]{:S(2)}) collective-permute-start(bf16[320,384]{1,0:T(8,128)(2,1)S(1)} %get-tuple-element.15), channel_id=1, source_target_pairs={{0,4},{2,6},{4,0},{6,2},{8,12},{10,14},{12,8},{14,10},{16,20},{18,... | collective-permute-start | bytes 737288 | tf_op jit(solution)/shard_map/ppermute | solution.py:399
  73.8 14.7 %collective-permute-start.23 = (bf16[320,384]{1,0:T(8,128)(2,1)S(1)}, bf16[320,384]{1,0:T(8,128)(2,1)}, u32[]{:S(2)}, u32[]{:S(2)}) collective-permute-start(bf16[320,384]{1,0:T(8,128)(2,1)S(1)} %get-tuple-element.13), channel_id=1, source_target_pairs={{0,12},{2,14},{4,8},{6,10},{8,4},{10,6},{12,0},{14,2},{16,28},{18,... | collective-permute-start | bytes 737288 | tf_op jit(solution)/shard_map/ppermute | solution.py:399
  76.1 12.5 %collective-permute-start.24 = (bf16[320,384]{1,0:T(8,128)(2,1)S(1)}, bf16[320,384]{1,0:T(8,128)(2,1)S(1)}, u32[]{:S(2)}, u32[]{:S(2)}) collective-permute-start(bf16[320,384]{1,0:T(8,128)(2,1)S(1)} %get-tuple-element.12), channel_id=1, source_target_pairs={{0,2},{2,0},{4,6},{6,4},{8,10},{10,8},{12,14},{14,12},{16,18},{18,... | collective-permute-start | bytes 737288 | tf_op jit(solution)/shard_map/ppermute | solution.py:399
  76.9 13.6 %collective-permute-start.12 = (bf16[320,384]{1,0:T(8,128)(2,1)S(1)}, bf16[320,384]{1,0:T(8,128)(2,1)S(1)}, u32[]{:S(2)}, u32[]{:S(2)}) collective-permute-start(bf16[320,384]{1,0:T(8,128)(2,1)S(1)} %get-tuple-element.19), channel_id=1, source_target_pairs={{0,4},{2,6},{4,0},{6,2},{8,12},{10,14},{12,8},{14,10},{16,20},{18,... | collective-permute-start | bytes 737288 | tf_op jit(solution)/shard_map/ppermute | solution.py:399
  85.3 13.7 %collective-permute-start.14 = (bf16[320,384]{1,0:T(8,128)(2,1)S(1)}, bf16[320,384]{1,0:T(8,128)(2,1)S(1)}, u32[]{:S(2)}, u32[]{:S(2)}) collective-permute-start(bf16[320,384]{1,0:T(8,128)(2,1)S(1)} %get-tuple-element.17), channel_id=1, source_target_pairs={{0,12},{2,14},{4,8},{6,10},{8,4},{10,6},{12,0},{14,2},{16,28},{18,... | collective-permute-start | bytes 737288 | tf_op jit(solution)/shard_map/ppermute | solution.py:399
  88.6 13.5 %collective-permute-start.15 = (bf16[320,384]{1,0:T(8,128)(2,1)}, bf16[320,384]{1,0:T(8,128)(2,1)}, u32[]{:S(2)}, u32[]{:S(2)}) collective-permute-start(bf16[320,384]{1,0:T(8,128)(2,1)} %get-tuple-element.16), channel_id=1, source_target_pairs={{0,2},{2,0},{4,6},{6,4},{8,10},{10,8},{12,14},{14,12},{16,18},{18,... | collective-permute-start | bytes 737288 | tf_op jit(solution)/shard_map/ppermute | solution.py:399
  89.3 13.9 %collective-permute-start.3 = (bf16[320,384]{1,0:T(8,128)(2,1)}, bf16[320,384]{1,0:T(8,128)(2,1)}, u32[]{:S(2)}, u32[]{:S(2)}) collective-permute-start(bf16[320,384]{1,0:T(8,128)(2,1)} %get-tuple-element.23), channel_id=1, source_target_pairs={{0,4},{2,6},{4,0},{6,2},{8,12},{10,14},{12,8},{14,10},{16,20},{18,... | collective-permute-start | bytes 737288 | tf_op jit(solution)/shard_map/ppermute | solution.py:399
  90.5 14.3 %collective-permute-start.25 = (bf16[320,384]{1,0:T(8,128)(2,1)}, bf16[320,384]{1,0:T(8,128)(2,1)}, u32[]{:S(2)}, u32[]{:S(2)}) collective-permute-start(bf16[320,384]{1,0:T(8,128)(2,1)} %collective-permute-done.21.refs_1_), channel_id=1, source_target_pairs={{0,2},{2,0},{4,6},{6,4},{8,10},{10,8},{12,14},{14,12},{16,18},{18,... | collective-permute-start | bytes 737288 | tf_op jit(solution)/shard_map/ppermute | solution.py:399
  102.0 15.4 %collective-permute-start.4 = (bf16[320,384]{1,0:T(8,128)(2,1)}, bf16[320,384]{1,0:T(8,128)(2,1)S(1)}, u32[]{:S(2)}, u32[]{:S(2)}) collective-permute-start(bf16[320,384]{1,0:T(8,128)(2,1)} %get-tuple-element.22), channel_id=1, source_target_pairs={{0,8},{2,10},{4,12},{6,14},{8,0},{10,2},{12,4},{14,6},{16,24},{18,... | collective-permute-start | bytes 737288 | tf_op jit(solution)/shard_map/ppermute | solution.py:399
  103.2 14.8 %collective-permute-start.5 = (bf16[320,384]{1,0:T(8,128)(2,1)}, bf16[320,384]{1,0:T(8,128)(2,1)S(1)}, u32[]{:S(2)}, u32[]{:S(2)}) collective-permute-start(bf16[320,384]{1,0:T(8,128)(2,1)} %get-tuple-element.21), channel_id=1, source_target_pairs={{0,12},{2,14},{4,8},{6,10},{8,4},{10,6},{12,0},{14,2},{16,28},{18,... | collective-permute-start | bytes 737288 | tf_op jit(solution)/shard_map/ppermute | solution.py:399
  104.8 13.3 %collective-permute-start.16 = (bf16[320,384]{1,0:T(8,128)(2,1)S(1)}, bf16[320,384]{1,0:T(8,128)(2,1)S(1)}, u32[]{:S(2)}, u32[]{:S(2)}) collective-permute-start(bf16[320,384]{1,0:T(8,128)(2,1)S(1)} %collective-permute-done.12.refs_1_), channel_id=1, source_target_pairs={{0,2},{2,0},{4,6},{6,4},{8,10},{10,8},{12,14},{14,12},{16,18},{18,... | collective-permute-start | bytes 737288 | tf_op jit(solution)/shard_map/ppermute | solution.py:399
  104.8 13.7 %collective-permute-start.17 = (bf16[320,384]{1,0:T(8,128)(2,1)S(1)}, bf16[320,384]{1,0:T(8,128)(2,1)S(1)}, u32[]{:S(2)}, u32[]{:S(2)}) collective-permute-start(bf16[320,384]{1,0:T(8,128)(2,1)S(1)} %collective-permute-done.13.refs_2_), channel_id=1, source_target_pairs={{0,2},{2,0},{4,6},{6,4},{8,10},{10,8},{12,14},{14,12},{16,18},{18,... | collective-permute-start | bytes 737288 | tf_op jit(solution)/shard_map/ppermute | solution.py:399
  105.3 13.3 %collective-permute-start.18 = (bf16[320,384]{1,0:T(8,128)(2,1)}, bf16[320,384]{1,0:T(8,128)(2,1)S(1)}, u32[]{:S(2)}, u32[]{:S(2)}) collective-permute-start(bf16[320,384]{1,0:T(8,128)(2,1)} %copy-done.5), channel_id=1, source_target_pairs={{0,2},{2,0},{4,6},{6,4},{8,10},{10,8},{12,14},{14,12},{16,18},{18,... | collective-permute-start | bytes 737288 | tf_op jit(solution)/shard_map/ppermute | solution.py:399
  118.6 18.0 %collective-permute-start.28 = (bf16[1280,128]{1,0:T(8,128)(2,1)S(1)}, bf16[1280,128]{1,0:T(8,128)(2,1)S(1)}, u32[]{:S(2)}, u32[]{:S(2)}) collective-permute-start(bf16[1280,128]{1,0:T(8,128)(2,1)S(1)} %shard_map.115.own_ref), channel_id=1, source_target_pairs={{0,2},{2,0},{4,6},{6,4},{8,10},{10,8},{12,14},{14,12},{16,18},{18,... | collective-permute-start | bytes 983048 | tf_op jit(solution)/shard_map/ppermute | solution.py:399
  127.4 14.9 %collective-permute-start.19 = (bf16[1280,128]{1,0:T(8,128)(2,1)S(1)}, bf16[1280,128]{1,0:T(8,128)(2,1)S(1)}, u32[]{:S(2)}, u32[]{:S(2)}) collective-permute-start(bf16[1280,128]{1,0:T(8,128)(2,1)S(1)} %shard_map.111.own_ref), channel_id=1, source_target_pairs={{0,2},{2,0},{4,6},{6,4},{8,10},{10,8},{12,14},{14,12},{16,18},{18,... | collective-permute-start | bytes 983048 | tf_op jit(solution)/shard_map/ppermute | solution.py:399
  139.6 32.4 %collective-permute-start.29 = (bf16[4,320,128]{2,1,0:T(8,128)(2,1)S(1)}, bf16[4,320,128]{2,1,0:T(8,128)(2,1)S(1)}, u32[]{:S(2)}, u32[]{:S(2)}) collective-permute-start(bf16[4,320,128]{2,1,0:T(8,128)(2,1)S(1)} %shard_map.117), channel_id=1, source_target_pairs={{0,16},{2,18},{4,20},{6,22},{8,24},{10,26},{12,28},{14,30},{16,0},... | collective-permute-start | bytes 983048 | tf_op jit(solution)/shard_map/ppermute | solution.py:399
  145.2 33.9 %collective-permute-start.20 = (bf16[4,320,128]{2,1,0:T(8,128)(2,1)S(1)}, bf16[4,320,128]{2,1,0:T(8,128)(2,1)S(1)}, u32[]{:S(2)}, u32[]{:S(2)}) collective-permute-start(bf16[4,320,128]{2,1,0:T(8,128)(2,1)S(1)} %shard_map.113), channel_id=1, source_target_pairs={{0,16},{2,18},{4,20},{6,22},{8,24},{10,26},{12,28},{14,30},{16,0},... | collective-permute-start | bytes 983048 | tf_op jit(solution)/shard_map/ppermute | solution.py:399
  148.5 36.9 %collective-permute-start.11 = (bf16[4,320,128]{2,1,0:T(8,128)(2,1)S(1)}, bf16[4,320,128]{2,1,0:T(8,128)(2,1)S(1)}, u32[]{:S(2)}, u32[]{:S(2)}) collective-permute-start(bf16[4,320,128]{2,1,0:T(8,128)(2,1)S(1)} %shard_map.109), channel_id=1, source_target_pairs={{0,16},{2,18},{4,20},{6,22},{8,24},{10,26},{12,28},{14,30},{16,0},... | collective-permute-start | bytes 983048 | tf_op jit(solution)/shard_map/ppermute | solution.py:399
  172.1 13.8 %collective-permute-start.32 = (bf16[320,128]{1,0:T(8,128)(2,1)S(1)}, bf16[320,128]{1,0:T(8,128)(2,1)S(1)}, u32[]{:S(2)}, u32[]{:S(2)}) collective-permute-start(bf16[320,128]{1,0:T(8,128)(2,1)S(1)} %get-tuple-element.26), channel_id=1, source_target_pairs={{0,4},{2,6},{4,0},{6,2},{8,12},{10,14},{12,8},{14,10},{16,20},{18,... | collective-permute-start | bytes 245768 | tf_op jit(solution)/shard_map/ppermute | solution.py:399
  172.9 15.0 %collective-permute-start.35 = (bf16[320,128]{1,0:T(8,128)(2,1)S(1)}, bf16[320,128]{1,0:T(8,128)(2,1)S(1)}, u32[]{:S(2)}, u32[]{:S(2)}) collective-permute-start(bf16[320,128]{1,0:T(8,128)(2,1)S(1)} %get-tuple-element.25), channel_id=1, source_target_pairs={{0,8},{2,10},{4,12},{6,14},{8,0},{10,2},{12,4},{14,6},{16,24},{18,... | collective-permute-start | bytes 245768 | tf_op jit(solution)/shard_map/ppermute | solution.py:399
  172.9 16.3 %collective-permute-start.38 = (bf16[320,128]{1,0:T(8,128)(2,1)S(1)}, bf16[320,128]{1,0:T(8,128)(2,1)S(1)}, u32[]{:S(2)}, u32[]{:S(2)}) collective-permute-start(bf16[320,128]{1,0:T(8,128)(2,1)S(1)} %get-tuple-element.24), channel_id=1, source_target_pairs={{0,12},{2,14},{4,8},{6,10},{8,4},{10,6},{12,0},{14,2},{16,28},{18,... | collective-permute-start | bytes 245768 | tf_op jit(solution)/shard_map/ppermute | solution.py:399
  201.2 23.0 %collective-permute-start.39 = (bf16[320,1536]{1,0:T(8,128)(2,1)S(1)}, bf16[320,1536]{1,0:T(8,128)(2,1)S(1)}, u32[]{:S(2)}, u32[]{:S(2)}) collective-permute-start(bf16[320,1536]{1,0:T(8,128)(2,1)S(1)} %shard_map.119), channel_id=1, source_target_pairs={{0,1},{1,0},{2,3},{3,2},{4,5},{5,4},{6,7},{7,6},{8,9},{9,8},{10,11... | collective-permute-start | bytes 2949128 | tf_op jit(solution)/shard_map/ppermute | solution.py:472
  (28 other events, 338.1 us)

commit v2 on v0

--- a/solution.py
+++ b/solution.py
@@ -1,6 +1,8 @@
 import jax
 import jax.numpy as jnp
 from jax import lax
+from jax.experimental import pallas as pl
+from jax.experimental.pallas import tpu as pltpu
 from jax.sharding import PartitionSpec as P
 
 HEAD_DIM = 128
@@ -8,6 +10,10 @@
 
 NEG = -1e30
 EPS = 1e-06
+MAXCLIP = 2560
+LOG2E = 1.4426950408889634
+MIB = 1024 * 1024
+COST = 1000000
 
 
 def clip_tables(total_rows, clip_lengths, prefix_lengths, noise_levels):
@@ -92,7 +98,7 @@
     return result
 
 
-def body(
+def gathered_body(
     inputs,
     norm_gain,
     level_table,
@@ -178,6 +184,287 @@
     return lax.psum_scatter(terms.astype(jnp.bfloat16), "head", scatter_dimension=1, tiled=True)
 
 
+def project_kernel(rows_ref, w_ref, *rest):
+    out_ref = rest[-1]
+    weights = jnp.concatenate([w_ref[0], w_ref[1], w_ref[2]], axis=1)
+    out_ref[0] = jnp.dot(
+        rows_ref[...], weights, preferred_element_type=jnp.float32
+    ).astype(jnp.bfloat16)
+
+
+def project_heads(normed, w_parts, first_head, count, group_heads, after):
+    rows, depth = normed.shape
+    return pl.pallas_call(
+        project_kernel,
+        grid=(4, count),
+        in_specs=[
+            pl.BlockSpec((rows, depth), lambda m, h: (0, 0)),
+            pl.BlockSpec(
+                (3, depth, HEAD_DIM), lambda m, h: (0, 0, group_heads * m + first_head + h)
+            ),
+        ]
+        + [pl.BlockSpec(memory_space=pl.ANY)] * len(after),
+        out_specs=pl.BlockSpec((1, rows, 3 * HEAD_DIM), lambda m, h: (m, 0, h)),
+        out_shape=jax.ShapeDtypeStruct((4, rows, count * 3 * HEAD_DIM), jnp.bfloat16),
+        compiler_params=pltpu.CompilerParams(vmem_limit_bytes=20 * MIB),
+        cost_estimate=pl.CostEstimate(flops=COST, bytes_accessed=COST, transcendentals=0),
+    )(normed, w_parts, *after)
+
+
+def attend_kernel(own_ref, pair_ref, query_mask_ref, key_mask_ref, *rest):
+    out_ref, q_all, k_all, v_all = rest[-4:]
+    slots, rows = own_ref.shape[:2]
+    tile = out_ref.shape[0]
+    step = pl.program_id(1)
+
+    @pl.when((pl.program_id(0) == 0) & (step == 0))
+    def _():
+        q_all[:, HEAD_DIM:] = query_mask_ref[...]
+        k_all[:, HEAD_DIM:] = key_mask_ref[...]
+
+    @pl.when(step == 0)
+    def _():
+        for index in range(2 * slots):
+            spot = slice(index * rows, (index + 1) * rows)
+            block = (own_ref if index < slots else pair_ref)[index % slots]
+            if index < slots:
+                q_all[spot, :HEAD_DIM] = block[:, :HEAD_DIM]
+            k_all[spot, :HEAD_DIM] = block[:, HEAD_DIM : 2 * HEAD_DIM]
+            v_all[spot, :] = block[:, 2 * HEAD_DIM :]
+
+    queries = q_all[pl.ds(pl.multiple_of(step * tile, tile), tile), :]
+    scores = lax.dot_general(
+        queries, k_all[...], (((1,), (1,)), ((), ())), preferred_element_type=jnp.float32
+    )
+    top = jnp.max(scores, axis=1, keepdims=True)
+    weights = jnp.exp2((scores - top) * (HEAD_DIM ** (-0.5) * LOG2E))
+    total = jnp.sum(weights, axis=1, keepdims=True)
+    summed = jnp.dot(weights.astype(jnp.bfloat16), v_all[...], preferred_element_type=jnp.float32)
+    out_ref[...] = (summed / total).astype(jnp.bfloat16)
+
+
+def attend(own, pair, query_mask, key_mask, count, after):
+    slots, rows = own.shape[:2]
+    keys, queries, tile = 2 * slots * rows, slots * rows, 256
+    width = 3 * HEAD_DIM
+    block = pl.BlockSpec((slots, rows, width), lambda h, t: (0, 0, h))
+    return pl.pallas_call(
+        attend_kernel,
+        grid=(count, queries // tile),
+        in_specs=[
+            block,
+            block,
+            pl.BlockSpec((queries, HEAD_DIM), lambda h, t: (0, 0)),
+            pl.BlockSpec((keys, HEAD_DIM), lambda h, t: (0, 0)),
+        ]
+        + [pl.BlockSpec(memory_space=pl.ANY)] * len(after),
+        out_specs=pl.BlockSpec((tile, HEAD_DIM), lambda h, t: (t, h)),
+        out_shape=jax.ShapeDtypeStruct((queries, count * HEAD_DIM), jnp.bfloat16),
+        scratch_shapes=[
+            pltpu.VMEM((queries, 2 * HEAD_DIM), jnp.bfloat16),
+            pltpu.VMEM((keys, 2 * HEAD_DIM), jnp.bfloat16),
+            pltpu.VMEM((keys, HEAD_DIM), jnp.bfloat16),
+        ],
+        compiler_params=pltpu.CompilerParams(vmem_limit_bytes=24 * MIB),
+        cost_estimate=pl.CostEstimate(flops=COST, bytes_accessed=COST, transcendentals=0),
+    )(own, pair, query_mask, key_mask, *after)
+
+
+def place_kernel(core_ref, own_ref, pair_ref, place_ref, out_ref):
+    rows = out_ref.shape[1]
+    half = own_ref.shape[0]
+    rank = 2 * pl.program_id(0) + core_ref[0]
+    wanted = rows * rank + lax.broadcasted_iota(jnp.int32, (rows, 1), 0)
+    picks = jnp.where(place_ref[...] == wanted, 1.0, 0.0).astype(jnp.bfloat16)
+    out_ref[0] = (
+        jnp.dot(picks[:, :half], own_ref[...], preferred_element_type=jnp.float32)
+        + jnp.dot(picks[:, half:], pair_ref[...], preferred_element_type=jnp.float32)
+    ).astype(jnp.bfloat16)
+
+
+def place_rows(core, own, pair, places, slots, rows):
+    half, width = own.shape
+    block = pl.BlockSpec((half, width), lambda n, core_ref: (0, 0))
+    return pl.pallas_call(
+        place_kernel,
+        grid_spec=pltpu.PrefetchScalarGridSpec(
+            num_scalar_prefetch=1,
+            grid=(slots,),
+            in_specs=[block, block, pl.BlockSpec((1, 2 * half), lambda n, core_ref: (0, 0))],
+            out_specs=pl.BlockSpec((1, rows, width), lambda n, core_ref: (n, 0, 0)),
+        ),
+        out_shape=jax.ShapeDtypeStruct((slots, rows, width), jnp.bfloat16),
+        compiler_params=pltpu.CompilerParams(vmem_limit_bytes=20 * MIB),
+        cost_estimate=pl.CostEstimate(flops=COST, bytes_accessed=COST, transcendentals=0),
+    )(core, own, pair, places)
+
+
+def out_kernel(side_ref, *refs):
+    w_ref, out_ref = refs[-2:]
+    columns = []
+    for m in range(4):
+        for ref in refs[:-2]:
+            columns.append(ref[m] + ref[4 + m])
+    rows = jnp.concatenate(columns, axis=1)
+    out_ref[...] = jnp.dot(rows, w_ref[...], preferred_element_type=jnp.float32).astype(
+        out_ref.dtype
+    )
+
+
+def project_out(parts, w_out, side, dtype):
+    rows = parts[0].shape[1]
+    depth = w_out.shape[0]
+    columns, tile = w_out.shape[1] // 2, 512
+    tiles = columns // tile
+    return pl.pallas_call(
+        out_kernel,
+        grid_spec=pltpu.PrefetchScalarGridSpec(
+            num_scalar_prefetch=1,
+            grid=(tiles,),
+            in_specs=[
+                pl.BlockSpec(part.shape, lambda t, side_ref: (0, 0, 0)) for part in parts
+            ]
+            + [pl.BlockSpec((depth, tile), lambda t, side_ref: (0, side_ref[0] * tiles + t))],
+            out_specs=pl.BlockSpec((rows, tile), lambda t, side_ref: (0, t)),
+        ),
+        out_shape=jax.ShapeDtypeStruct((rows, columns), dtype),
+        compiler_params=pltpu.CompilerParams(vmem_limit_bytes=20 * MIB),
+        cost_estimate=pl.CostEstimate(flops=COST, bytes_accessed=COST, transcendentals=0),
+    )(side.reshape(1), *parts, w_out)
+
+
+def row_facts(rows, clip_lengths, prefix_lengths, noise_levels):
+    ends = jnp.cumsum(clip_lengths)
+    begins = ends - clip_lengths
+    lead = begins + jnp.minimum(prefix_lengths, clip_lengths)
+    past = rows[:, None] >= ends[None, :]
+    clip = jnp.sum(past.astype(jnp.int32), axis=1)
+    inside = (rows[:, None] >= begins[None, :]) & jnp.logical_not(past)
+    in_prefix = jnp.any(inside & (rows[:, None] < lead[None, :]), axis=1)
+    level = jnp.sum(jnp.where(inside, noise_levels[None, :], 0), axis=1)
+    return clip, in_prefix, level
+
+
+CHUNKS = ((0, 1), (1, 1), (2, 1))
+SWAP_ROWS = (160, 160)
+
+
+def halved_body(
+    inputs,
+    norm_gain,
+    level_table,
+    w_qkv,
+    w_out,
+    clip_lengths,
+    prefix_lengths,
+    noise_levels,
+    token_rank,
+):
+    rank_here = lax.axis_index("ctx")
+    side = lax.axis_index("head")
+    per_dev = inputs.shape[0]
+    ranks = 16
+    half_rows = 8 * per_dev
+    local_width = w_qkv.shape[2]
+    group_heads = local_width // HEAD_DIM // 4
+    clips = clip_lengths.shape[0]
+    half, block, core = rank_here // 8, rank_here % 8, rank_here % 2
+    half_groups = [[8 * h + 2 * m + c for m in range(4)] for h in range(2) for c in range(2)]
+    core_groups = [[2 * n + c for n in range(8)] for c in range(2)]
+
+    def spread(array, groups):
+        return lax.all_to_all(array, "ctx", 0, 0, axis_index_groups=groups, tiled=True)
+
+    def with_pair(array):
+        return lax.ppermute(array, "ctx", [(r, r ^ 1) for r in range(ranks)])
+
+    begins = jnp.cumsum(clip_lengths) - clip_lengths
+    start = jnp.sum(jnp.where(clip_lengths == MAXCLIP, begins, 0))
+    early = start <= half_rows // 2
+
+    def packed_row(spots):
+        swapped = jnp.where(early, spots < start, spots >= start)
+        return spots + half_rows * (half ^ swapped.astype(jnp.int32)), swapped
+
+    own_packed, own_swapped = packed_row(block * per_dev + jnp.arange(per_dev, dtype=jnp.int32))
+
+    def gather_rows(blocks):
+        def run(rows, swapped):
+            pairs = [(r, r ^ 8) for r in range(ranks) if r % 8 in blocks]
+            bounds = [sum(SWAP_ROWS[:i]) for i in range(len(SWAP_ROWS) + 1)]
+            cuts = list(zip(bounds[:-1], bounds[1:]))
+            moved = [lax.ppermute(rows[low:high], "ctx", pairs) for low, high in cuts]
+            kept = [
+                jnp.where(swapped[low:high, None], part, rows[low:high])
+                for part, (low, high) in zip(moved, cuts)
+            ]
+            other = [lax.ppermute(part, "head", [(0, 1), (1, 0)]) for part in kept]
+            return tuple(kept), tuple(other)
+
+        return run
+
+    kept, other = lax.cond(
+        early, gather_rows(range(4)), gather_rows(range(4, 8)), inputs, own_swapped
+    )
+    rows, other = jnp.concatenate(kept, axis=0), jnp.concatenate(other, axis=0)
+    full_rows = jnp.where(
+        side == 0,
+        jnp.concatenate([rows, other], axis=1),
+        jnp.concatenate([other, rows], axis=1),
+    )
+    unused, own_prefix, own_level = row_facts(
+        own_packed, clip_lengths, prefix_lengths, noise_levels
+    )
+    normed = normalize(full_rows, own_prefix, own_level, level_table, norm_gain)
+
+    order = jnp.concatenate([2 * jnp.arange(4) + core, 2 * jnp.arange(4) + 1 - core]).astype(
+        jnp.int32
+    )
+    spots = (order[:, None] * per_dev + jnp.arange(per_dev, dtype=jnp.int32)[None, :]).reshape(-1)
+    packed, unused = packed_row(spots)
+    clip, in_prefix, unused = row_facts(packed, clip_lengths, prefix_lengths, noise_levels)
+    column = jnp.arange(HEAD_DIM, dtype=jnp.int32)[None, :]
+    same = column == clip[:, None]
+    last = column == clips
+    own_rows = half_rows // 2
+    query_mask = jnp.where(
+        same[:own_rows] | (last & in_prefix[:own_rows, None]), 1.0, 0.0
+    ).astype(jnp.bfloat16)
+    key_mask = jnp.where(
+        ((column < clips) & jnp.logical_not(same)) | (last & jnp.logical_not(in_prefix)[:, None]),
+        NEG,
+        0.0,
+    ).astype(jnp.bfloat16)
+
+    within, unused, unused = rank_tables(token_rank, ranks, per_dev)
+    place = token_rank * per_dev + within
+    every_packed, unused = packed_row(jnp.arange(half_rows, dtype=jnp.int32))
+    half_place = jnp.where(every_packed >= half_rows, place[half_rows:], place[:half_rows])
+    half_place = half_place.reshape(4, 2, per_dev)
+    places = jnp.where(
+        core == 0,
+        jnp.concatenate([half_place[:, 0], half_place[:, 1]], axis=0),
+        jnp.concatenate([half_place[:, 1], half_place[:, 0]], axis=0),
+    ).reshape(1, half_rows)
+
+    w_parts = jnp.transpose(w_qkv, (1, 0, 2))
+    arrived, after = [], []
+    for first_head, count in CHUNKS:
+        mine = project_heads(normed, w_parts, first_head, count, group_heads, [])
+        arrived.append(spread(mine, half_groups))
+    parts = []
+    for (first_head, count), own in zip(CHUNKS, arrived):
+        result = attend(own, with_pair(own), query_mask, key_mask, count, after)
+        placed = place_rows(core.reshape(1), result, with_pair(result), places, 8, per_dev)
+        after = [placed]
+        parts.append(spread(placed, core_groups))
+
+    away = project_out(parts, w_out, 1 - side, jnp.bfloat16)
+    away = lax.ppermute(away, "head", [(0, 1), (1, 0)])
+    stay = project_out(parts, w_out, side, jnp.float32)
+    return (stay + away.astype(jnp.float32)).astype(jnp.bfloat16)
+
+
 def solution(mesh):
     in_specs = (
         P("ctx", "head"),
@@ -191,4 +478,17 @@
         P(),
     )
     out_specs = P("ctx", "head")
+
+    def body(inputs, norm_gain, level_table, w_qkv, *rest):
+        ranks, sides = mesh.shape["ctx"], mesh.shape["head"]
+        heads_here = w_qkv.shape[2] // HEAD_DIM
+        halved = (
+            ranks == 16
+            and sides == 2
+            and ranks * inputs.shape[0] == 2 * MAXCLIP
+            and heads_here % 4 == 0
+        )
+        run = halved_body if halved else gathered_body
+        return run(inputs, norm_gain, level_table, w_qkv, *rest)
+
     return jax.shard_map(body, mesh=mesh, in_specs=in_specs, out_specs=out_specs, check_vma=False)

time: 536 us -> 251 us (0.47); the launches traced: 528 us -> 249 us
  matrix products: 151 us -> 1.06 us
  local copies, waits for them, and re-layouts: 138 us -> 42.1 us
  waiting for transfers between devices: 172 us -> 81.2 us
  Pallas kernels: 0 us -> 64.7 us
  starting transfers between devices: 7.47 us -> 39.1 us
  other arithmetic: 45 us -> 20.3 us
  between operations: 14.1 us -> 0.93 us
    dot_general x26 -> x0, matrix products: 149 us -> none  [the longest x12 85.3 us: absorb(): lax.dot_general(q_head, k_head, (((1,), (1,)), ((), ())), preferred_eleme...]
    all_gather x2 -> x0, waiting for transfers between devices: 103 us -> none  [the longest x1 103 us: body(): lax.all_gather(pairs, 'ctx', axis=0, tiled=True)]
    gather x5 -> x0, local copies, waits for them, and re-layouts: 66.5 us -> none  [the longest x1 32.4 us: body(): key_prefix = in_prefix[order]]
    pallas_call x0 -> x11, Pallas kernels: none -> 64.7 us  [the longest x3 24.1 us: attend(): pl.pallas_call(attend_kernel, grid=(count, queries // tile), in_specs=[bl...]
    ppermute x0 -> x11, waiting for transfers between devices: none -> 59.8 us  [the longest x2 21.2 us: run(): other = [lax.ppermute(part, 'head', [(0, 1), (1, 0)]) for part in kept]]
    scatter x3 -> x0, local copies, waits for them, and re-layouts: 30.8 us -> none  [the longest x1 19.6 us: body(): jnp.zeros((total_rows,), jnp.int32).at[place]]
    reduce_scatter x1 -> x0, waiting for transfers between devices: 30.5 us -> none  [body(): lax.psum_scatter(terms.astype(jnp.bfloat16), 'head', scatter_dimension=1,...]
    reduce_sum x5 -> x2, other arithmetic: 26.9 us -> 0.19 us  [the longest x1 0.1 us: row_facts(): clip = jnp.sum(past.astype(jnp.int32), axis=1)]
  transfers between devices with their start and end apart: 4 -> 17, of which waited for: 3 -> 11; matrix products, arithmetic and copies ran while one was open for 23% -> 6% of each run, Pallas kernels for 0% -> 22%
where the time goes in v2:
time: 251 us; the launch traced here: 249 us
  waiting for transfers between devices  81.2 us (32%)
  Pallas kernels  64.7 us (26%)
  local copies, waits for them, and re-layouts  42.1 us (17%)
  starting transfers between devices  39.1 us (16%)
  other arithmetic  20.3 us (8%)
    unnamed x28, local copies, waits for them, and re-layouts  38.7 us
    all_to_all x6, starting transfers between devices, spread(): lax.all_to_all(array, 'ctx', 0, 0, axis_index_groups=groups, tiled=True)  26.2 us
    pallas_call x3, Pallas kernels, attend(): pl.pallas_call(attend_kernel, grid=(count, queries // tile), in_specs=[bl...  24.1 us
    all_to_all x6, waiting for transfers between devices, spread(): lax.all_to_all(array, 'ctx', 0, 0, axis_index_groups=groups, tiled=True)  21.3 us
    ppermute x2, waiting for transfers between devices, run(): other = [lax.ppermute(part, 'head', [(0, 1), (1, 0)]) for part in kept]  21.2 us
    ppermute x2, waiting for transfers between devices, run(): moved = [lax.ppermute(rows[low:high], 'ctx', pairs) for low, high in cuts]  19.7 us
    pallas_call x3, Pallas kernels, project_heads(): pl.pallas_call(project_kernel, grid=(4, count), in_specs=[pl.BlockSpec((r...  19.2 us
    pallas_call x3, Pallas kernels, place_rows(): pl.pallas_call(place_kernel, grid_spec=pltpu.PrefetchScalarGridSpec(num_s...  16.5 us
  transfers between devices with their start and end apart: 17, of which 11 were waited for; matrix products, arithmetic and copies ran while one was open for 6% of the time, Pallas kernels for 22%

profile of v2, /device:TPU:0, one launch (start us, length us, event | category | flops | bytes accessed | tf_op | source)
XLA Modules:
  0.0 249.3 jit_solution(4586644925714795220)
XLA Ops:
  3.3 53.4 %conditional.1 = (bf16[160,1536]{1,0:T(8,128)(2,1)}, bf16[160,1536]{1,0:T(8,128)(2,1)}, bf16[160,1536]{1,0:T(8,128)(2,1)}, bf16[160,1536]{1,0:T(8,128)(2,1)}) conditional(s32[]{:T(128)} %convert_element_type.50, (pred[320]{0:T(512)(128)(4,1)S(1)}, bf16[320,1536]{1,0:T(8,128)(2,1)}) %tuple.13, (pred[320]{0:T(512)(128)(4,1)S(1)}, ...), branch_computations={%region_2.3_spmd, %region_3.4_spmd} | conditional | flops 491520 | bytes 16712860 | solution.py:406
  4.7 5.9 %collective-permute-start.4 = (bf16[160,1536]{1,0:T(8,128)(2,1)S(1)}, bf16[160,1536]{1,0:T(8,128)(2,1)S(1)}, u32[]{:S(2)}, u32[]{:S(2)}) collective-permute-start(bf16[160,1536]{1,0:T(8,128)(2,1)S(1)} %get-tuple-element.36), channel_id=1, source_target_pairs={{0,16},{2,18},{4,20},{6,22},{16,0},{18,2},{20,4},{22,6},{1,17},{3,... | collective-permute-start | bytes 1474568 | tf_op jit(solution)/shard_map/cond/branch_1_fun/ppermute | solution.py:396
  12.6 10.0 %collective-permute-done.4 = bf16[160,1536]{1,0:T(8,128)(2,1)S(1)} collective-permute-done((bf16[160,1536]{1,0:T(8,128)(2,1)S(1)}, bf16[160,1536]{1,0:T(8,128)(2,1)S(1)}, u32[]{:S(2)}, u32[]{:S(2)}) %collective-permute-start.4) | collective-permute-done | bytes 491552 | tf_op jit(solution)/shard_map/cond/branch_1_fun/ppermute | solution.py:396
  22.7 9.7 %collective-permute-done.5 = bf16[160,1536]{1,0:T(8,128)(2,1)S(1)} collective-permute-done((bf16[160,1536]{1,0:T(8,128)(2,1)S(1)}, bf16[160,1536]{1,0:T(8,128)(2,1)S(1)}, u32[]{:S(2)}, u32[]{:S(2)}) %collective-permute-start.5) | collective-permute-done | bytes 491552 | tf_op jit(solution)/shard_map/cond/branch_1_fun/ppermute | solution.py:396
  35.5 12.4 %collective-permute-done.6 = bf16[160,1536]{1,0:T(8,128)(2,1)} collective-permute-done((bf16[160,1536]{1,0:T(8,128)(2,1)}, bf16[160,1536]{1,0:T(8,128)(2,1)}, u32[]{:S(2)}, u32[]{:S(2)}) %collective-permute-start.6) | collective-permute-done | bytes 491552 | tf_op jit(solution)/shard_map/cond/branch_1_fun/ppermute | solution.py:401
  47.9 8.8 %collective-permute-done.7 = bf16[160,1536]{1,0:T(8,128)(2,1)} collective-permute-done((bf16[160,1536]{1,0:T(8,128)(2,1)}, bf16[160,1536]{1,0:T(8,128)(2,1)}, u32[]{:S(2)}, u32[]{:S(2)}) %collective-permute-start.7) | collective-permute-done | bytes 491552 | tf_op jit(solution)/shard_map/cond/branch_1_fun/ppermute | solution.py:401
  62.0 9.0 %copy-done.2 = bf16[3072,3,1536]{2,0,1:T(8,128)(2,1)S(1)} copy-done((bf16[3072,3,1536]{2,0,1:T(8,128)(2,1)S(1)}, bf16[3072,3,1536]{2,0,1:T(8,128)(2,1)}, u32[]{:S(2)}) %copy-start.2) | copy-done | bytes 28311576
  71.0 6.4 %shard_map.91 = bf16[4,320,384]{2,1,0:T(8,128)(2,1)S(1)} custom-call(bf16[320,3072]{1,0:T(8,128)(2,1)S(1)} %multiply_convert_fusion.rows_ref, bf16[3,3072,1536]{2,1,0:T(8,128)(2,1)S(1)} %bitcast.35), custom_call_target="tpu_custom_call" | custom-call | flops 1000000 | bytes 1000000 | tf_op jit(solution)/shard_map/pallas_call | solution.py:197
  83.1 8.4 %reduce-window.19 = s32[16,40,128]{2,1,0:T(8,128)S(1)} reduce-window(s32[16,40,128]{2,1,0:T(8,128)} %fusion.3, s32[]{:T(128)} %constant.70.clone.1), window={size=1x1x128 pad=0_0x0_0x127_0}, to_apply=%region_9.10 | reduce-window | flops 10403840 | bytes 655364 | tf_op jit(solution)/shard_map/reduce-window.1
  92.1 9.1 %copy-done.3 = bf16[3072,3,1536]{2,0,1:T(8,128)(2,1)S(1)} copy-done((bf16[3072,3,1536]{2,0,1:T(8,128)(2,1)S(1)}, bf16[3072,3,1536]{2,0,1:T(8,128)(2,1)}, u32[]{:S(2)}) %copy-start.3) | copy-done | bytes 28311576
  101.2 6.4 %shard_map.94 = bf16[4,320,384]{2,1,0:T(8,128)(2,1)S(1)} custom-call(bf16[320,3072]{1,0:T(8,128)(2,1)S(1)} %multiply_convert_fusion.rows_ref, bf16[3,3072,1536]{2,1,0:T(8,128)(2,1)S(1)} %bitcast.36), custom_call_target="tpu_custom_call" | custom-call | flops 1000000 | bytes 1000000 | tf_op jit(solution)/shard_map/pallas_call | solution.py:197
  108.6 4.2 %all-to-all-start.2 = ((bf16[4,320,384]{2,1,0:T(8,128)(2,1)}), bf16[4,320,384]{2,1,0:T(8,128)(2,1)}, u32[]{:S(2)}, u32[]{:S(2)}) async-start(bf16[4,320,384]{2,1,0:T(8,128)(2,1)} %copy-done.9), calls=%async_computation.2 | async-start | bytes 1966080 | tf_op jit(solution)/shard_map/all_to_all | solution.py:376
  113.2 9.1 %copy-done.4 = bf16[3072,3,1536]{2,0,1:T(8,128)(2,1)S(1)} copy-done((bf16[3072,3,1536]{2,0,1:T(8,128)(2,1)S(1)}, bf16[3072,3,1536]{2,0,1:T(8,128)(2,1)}, u32[]{:S(2)}) %copy-start.4) | copy-done | bytes 28311576
  122.2 6.4 %shard_map.97 = bf16[4,320,384]{2,1,0:T(8,128)(2,1)S(1)} custom-call(bf16[320,3072]{1,0:T(8,128)(2,1)S(1)} %multiply_convert_fusion.rows_ref, bf16[3,3072,1536]{2,1,0:T(8,128)(2,1)S(1)} %bitcast.37), custom_call_target="tpu_custom_call" | custom-call | flops 1000000 | bytes 1000000 | tf_op jit(solution)/shard_map/pallas_call | solution.py:197
  131.2 4.2 %all-to-all-start.4 = ((bf16[4,320,384]{2,1,0:T(8,128)(2,1)}), bf16[4,320,384]{2,1,0:T(8,128)(2,1)}, u32[]{:S(2)}, u32[]{:S(2)}) async-start(bf16[4,320,384]{2,1,0:T(8,128)(2,1)} %copy-done.7), calls=%async_computation.4 | async-start | bytes 1966080 | tf_op jit(solution)/shard_map/all_to_all | solution.py:376
  138.5 7.0 %shard_map.92.own_ref = bf16[1280,128]{1,0:T(8,128)(2,1)S(1)} custom-call(bf16[4,320,384]{2,1,0:T(8,128)(2,1)S(1)} %all-to-all-done.own_ref, bf16[4,320,384]{2,1,0:T(8,128)(2,1)S(1)} %collective-permute-done.8.pair_ref, bf16[1280,128]{1,0:T(8,128)(2,1)S(1)} %select_convert_fusion.1.query_mask_ref, bf16[2560,128]{1,0:T(8,128)(2,1)S(1)} %select_convert_fusion.key_mask_ref), custom_call_target="tpu_custom_call" | custom-call | flops 1000000 | bytes 1000000 | tf_op jit(solution)/shard_map/pallas_call | solution.py:251
  147.2 5.5 %shard_map.93.rest_0_ = bf16[8,320,128]{2,1,0:T(8,128)(2,1)} custom-call(s32[1]{0:T(128)} %bitcast.1.core_ref, bf16[1280,128]{1,0:T(8,128)(2,1)S(1)} %shard_map.92.own_ref, bf16[1280,128]{1,0:T(8,128)(2,1)S(1)} %collective-permute-done.9.pair_ref, s32[1,2560]{1,0:T(1,128)S(1)} %select_n.124.place_ref), custom_call_target="tpu_custom_call" | custom-call | flops 1000000 | bytes 1000000 | tf_op jit(solution)/shard_map/pallas_call | solution.py:288
  152.7 5.9 %all-to-all-start.1 = ((bf16[8,320,128]{2,1,0:T(8,128)(2,1)}), bf16[8,320,128]{2,1,0:T(8,128)(2,1)S(1)}, u32[]{:S(2)}, u32[]{:S(2)}) async-start(bf16[8,320,128]{2,1,0:T(8,128)(2,1)} %shard_map.93.rest_0_), calls=%async_computation.1 | async-start | bytes 1310720 | tf_op jit(solution)/shard_map/all_to_all | solution.py:376
  158.6 8.5 %shard_map.95.own_ref = bf16[1280,128]{1,0:T(8,128)(2,1)S(1)} custom-call(bf16[4,320,384]{2,1,0:T(8,128)(2,1)} %all-to-all-done.2.own_ref, bf16[4,320,384]{2,1,0:T(8,128)(2,1)} %collective-permute-done.10.pair_ref, bf16[1280,128]{1,0:T(8,128)(2,1)S(1)} %select_convert_fusion.1.query_mask_ref, bf16[2560,128]{1,0:T(8,128)(2,1)S(1)} %select_convert_fusion.key_mask_ref, ...), custom_call_target="tpu_custom_call" | custom-call | flops 1000000 | bytes 1000000 | tf_op jit(solution)/shard_map/pallas_call | solution.py:251
  168.8 5.5 %shard_map.96.rest_0_ = bf16[8,320,128]{2,1,0:T(8,128)(2,1)} custom-call(s32[1]{0:T(128)} %bitcast.1.core_ref, bf16[1280,128]{1,0:T(8,128)(2,1)S(1)} %shard_map.95.own_ref, bf16[1280,128]{1,0:T(8,128)(2,1)S(1)} %collective-permute-done.11.pair_ref, s32[1,2560]{1,0:T(1,128)S(1)} %select_n.124.place_ref), custom_call_target="tpu_custom_call" | custom-call | flops 1000000 | bytes 1000000 | tf_op jit(solution)/shard_map/pallas_call | solution.py:288
  180.3 8.5 %shard_map.98.own_ref = bf16[1280,128]{1,0:T(8,128)(2,1)S(1)} custom-call(bf16[4,320,384]{2,1,0:T(8,128)(2,1)} %all-to-all-done.4.own_ref, bf16[4,320,384]{2,1,0:T(8,128)(2,1)} %collective-permute-done.12.pair_ref, bf16[1280,128]{1,0:T(8,128)(2,1)S(1)} %select_convert_fusion.1.query_mask_ref, bf16[2560,128]{1,0:T(8,128)(2,1)S(1)} %select_convert_fusion.key_mask_ref, ...), custom_call_target="tpu_custom_call" | custom-call | flops 1000000 | bytes 1000000 | tf_op jit(solution)/shard_map/pallas_call | solution.py:251
  190.6 5.5 %shard_map.99 = bf16[8,320,128]{2,1,0:T(8,128)(2,1)} custom-call(s32[1]{0:T(128)} %bitcast.1.core_ref, bf16[1280,128]{1,0:T(8,128)(2,1)S(1)} %shard_map.98.own_ref, bf16[1280,128]{1,0:T(8,128)(2,1)S(1)} %collective-permute-done.13.pair_ref, s32[1,2560]{1,0:T(1,128)S(1)} %select_n.124.place_ref), custom_call_target="tpu_custom_call" | custom-call | flops 1000000 | bytes 1000000 | tf_op jit(solution)/shard_map/pallas_call | solution.py:288
  202.0 17.6 %all-to-all-done.5.refs_2_ = bf16[8,320,128]{2,1,0:T(8,128)(2,1)S(1)} async-done(((bf16[8,320,128]{2,1,0:T(8,128)(2,1)}), bf16[8,320,128]{2,1,0:T(8,128)(2,1)S(1)}, u32[]{:S(2)}, u32[]{:S(2)}) %all-to-all-start.5) | async-done | bytes 655392 | tf_op jit(solution)/shard_map/all_to_all | solution.py:376
  233.5 14.6 %collective-permute-done.14 = bf16[320,1536]{1,0:T(8,128)(2,1)S(1)} collective-permute-done((bf16[320,1536]{1,0:T(8,128)(2,1)S(1)}, bf16[320,1536]{1,0:T(8,128)(2,1)S(1)}, u32[]{:S(2)}, u32[]{:S(2)}) %collective-permute-start.14) | collective-permute-done | bytes 983072 | tf_op jit(solution)/shard_map/ppermute | solution.py:463
  (93 shorter events, 59.5 us)
Async XLA Ops:
  0.0 60.3 %copy-start = (bf16[8,3072]{1,0:T(8,128)(2,1)S(1)}, bf16[8,3072]{1,0:T(8,128)(2,1)}, u32[]{:S(2)}) copy-start(bf16[8,3072]{1,0:T(8,128)(2,1)} %param.13) | copy-start | bytes 147460
  3.3 29.0 %copy-start.11 = (bf16[320,1536]{1,0:T(8,128)(2,1)S(1)}, bf16[320,1536]{1,0:T(8,128)(2,1)}, u32[]{:S(2)}) copy-start(bf16[320,1536]{1,0:T(8,128)(2,1)} %get-tuple-element.16) | copy-start | bytes 2949124 | tf_op jit(solution)/shard_map/cond
  4.7 18.0 %collective-permute-start.4 = (bf16[160,1536]{1,0:T(8,128)(2,1)S(1)}, bf16[160,1536]{1,0:T(8,128)(2,1)S(1)}, u32[]{:S(2)}, u32[]{:S(2)}) collective-permute-start(bf16[160,1536]{1,0:T(8,128)(2,1)S(1)} %get-tuple-element.36), channel_id=1, source_target_pairs={{0,16},{2,18},{4,20},{6,22},{16,0},{18,2},{20,4},{22,6},{1,17},{3,... | collective-permute-start | bytes 1474568 | tf_op jit(solution)/shard_map/cond/branch_1_fun/ppermute | solution.py:396
  10.6 21.7 %collective-permute-start.5 = (bf16[160,1536]{1,0:T(8,128)(2,1)S(1)}, bf16[160,1536]{1,0:T(8,128)(2,1)S(1)}, u32[]{:S(2)}, u32[]{:S(2)}) collective-permute-start(bf16[160,1536]{1,0:T(8,128)(2,1)S(1)} %get-tuple-element.35), channel_id=1, source_target_pairs={{0,16},{2,18},{4,20},{6,22},{16,0},{18,2},{20,4},{22,6},{1,17},{3,... | collective-permute-start | bytes 1474568 | tf_op jit(solution)/shard_map/cond/branch_1_fun/ppermute | solution.py:396
  33.5 14.5 %collective-permute-start.6 = (bf16[160,1536]{1,0:T(8,128)(2,1)}, bf16[160,1536]{1,0:T(8,128)(2,1)}, u32[]{:S(2)}, u32[]{:S(2)}) collective-permute-start(bf16[160,1536]{1,0:T(8,128)(2,1)} %get-tuple-element.60), channel_id=1, source_target_pairs={{0,1},{1,0},{2,3},{3,2},{4,5},{5,4},{6,7},{7,6},{8,9},{9,8},{10,11... | collective-permute-start | bytes 1474568 | tf_op jit(solution)/shard_map/cond/branch_1_fun/ppermute | solution.py:401
  35.0 21.7 %collective-permute-start.7 = (bf16[160,1536]{1,0:T(8,128)(2,1)}, bf16[160,1536]{1,0:T(8,128)(2,1)}, u32[]{:S(2)}, u32[]{:S(2)}) collective-permute-start(bf16[160,1536]{1,0:T(8,128)(2,1)} %get-tuple-element.61), channel_id=1, source_target_pairs={{0,1},{1,0},{2,3},{3,2},{4,5},{5,4},{6,7},{7,6},{8,9},{9,8},{10,11... | collective-permute-start | bytes 1474568 | tf_op jit(solution)/shard_map/cond/branch_1_fun/ppermute | solution.py:401
  62.0 9.1 %copy-start.2 = (bf16[3072,3,1536]{2,0,1:T(8,128)(2,1)S(1)}, bf16[3072,3,1536]{2,0,1:T(8,128)(2,1)}, u32[]{:S(2)}) copy-start(bf16[3072,3,1536]{2,0,1:T(8,128)(2,1)} %param.14) | copy-start | bytes 84934656
  78.4 3.9 %copy-start.12 = (s32[5120]{0:T(1024)S(1)}, s32[5120]{0:T(1024)}, u32[]{:S(2)}) copy-start(s32[5120]{0:T(1024)} %param.19) | copy-start | bytes 61444
  78.4 30.2 %all-to-all-start = ((bf16[4,320,384]{2,1,0:T(8,128)(2,1)}), bf16[4,320,384]{2,1,0:T(8,128)(2,1)S(1)}, u32[]{:S(2)}, u32[]{:S(2)}) async-start(bf16[4,320,384]{2,1,0:T(8,128)(2,1)} %copy-done.8), calls=%async_computation | async-start | bytes 1966080 | tf_op jit(solution)/shard_map/all_to_all | solution.py:376
  92.1 9.1 %copy-start.3 = (bf16[3072,3,1536]{2,0,1:T(8,128)(2,1)S(1)}, bf16[3072,3,1536]{2,0,1:T(8,128)(2,1)}, u32[]{:S(2)}) copy-start(bf16[3072,3,1536]{2,0,1:T(8,128)(2,1)} %param.14) | copy-start | bytes 84934656
  108.6 22.6 %all-to-all-start.2 = ((bf16[4,320,384]{2,1,0:T(8,128)(2,1)}), bf16[4,320,384]{2,1,0:T(8,128)(2,1)}, u32[]{:S(2)}, u32[]{:S(2)}) async-start(bf16[4,320,384]{2,1,0:T(8,128)(2,1)} %copy-done.9), calls=%async_computation.2 | async-start | bytes 1966080 | tf_op jit(solution)/shard_map/all_to_all | solution.py:376
  113.2 9.1 %copy-start.4 = (bf16[3072,3,1536]{2,0,1:T(8,128)(2,1)S(1)}, bf16[3072,3,1536]{2,0,1:T(8,128)(2,1)}, u32[]{:S(2)}) copy-start(bf16[3072,3,1536]{2,0,1:T(8,128)(2,1)} %param.14) | copy-start | bytes 84934656
  131.1 7.4 %collective-permute-start.8 = (bf16[4,320,384]{2,1,0:T(8,128)(2,1)S(1)}, bf16[4,320,384]{2,1,0:T(8,128)(2,1)S(1)}, u32[]{:S(2)}, u32[]{:S(2)}) collective-permute-start(bf16[4,320,384]{2,1,0:T(8,128)(2,1)S(1)} %all-to-all-done.own_ref), channel_id=1, source_target_pairs={{0,2},{2,0},{4,6},{6,4},{8,10},{10,8},{12,14},{14,12},{16,18},{18,... | collective-permute-start | bytes 2949128 | tf_op jit(solution)/shard_map/ppermute | solution.py:379
  131.2 21.5 %all-to-all-start.4 = ((bf16[4,320,384]{2,1,0:T(8,128)(2,1)}), bf16[4,320,384]{2,1,0:T(8,128)(2,1)}, u32[]{:S(2)}, u32[]{:S(2)}) async-start(bf16[4,320,384]{2,1,0:T(8,128)(2,1)} %copy-done.7), calls=%async_computation.4 | async-start | bytes 1966080 | tf_op jit(solution)/shard_map/all_to_all | solution.py:376
  138.0 20.6 %collective-permute-start.10 = (bf16[4,320,384]{2,1,0:T(8,128)(2,1)}, bf16[4,320,384]{2,1,0:T(8,128)(2,1)}, u32[]{:S(2)}, u32[]{:S(2)}) collective-permute-start(bf16[4,320,384]{2,1,0:T(8,128)(2,1)} %all-to-all-done.2.own_ref), channel_id=1, source_target_pairs={{0,2},{2,0},{4,6},{6,4},{8,10},{10,8},{12,14},{14,12},{16,18},{18,... | collective-permute-start | bytes 2949128 | tf_op jit(solution)/shard_map/ppermute | solution.py:379
  145.5 1.7 collective-permute-start.9
  152.7 23.5 %all-to-all-start.1 = ((bf16[8,320,128]{2,1,0:T(8,128)(2,1)}), bf16[8,320,128]{2,1,0:T(8,128)(2,1)S(1)}, u32[]{:S(2)}, u32[]{:S(2)}) async-start(bf16[8,320,128]{2,1,0:T(8,128)(2,1)} %shard_map.93.rest_0_), calls=%async_computation.1 | async-start | bytes 1310720 | tf_op jit(solution)/shard_map/all_to_all | solution.py:376
  167.2 1.7 collective-permute-start.11
  167.2 13.1 %collective-permute-start.12 = (bf16[4,320,384]{2,1,0:T(8,128)(2,1)}, bf16[4,320,384]{2,1,0:T(8,128)(2,1)}, u32[]{:S(2)}, u32[]{:S(2)}) collective-permute-start(bf16[4,320,384]{2,1,0:T(8,128)(2,1)} %all-to-all-done.4.own_ref), channel_id=1, source_target_pairs={{0,2},{2,0},{4,6},{6,4},{8,10},{10,8},{12,14},{14,12},{16,18},{18,... | collective-permute-start | bytes 2949128 | tf_op jit(solution)/shard_map/ppermute | solution.py:379
  176.2 21.7 %all-to-all-start.3 = ((bf16[8,320,128]{2,1,0:T(8,128)(2,1)}), bf16[8,320,128]{2,1,0:T(8,128)(2,1)S(1)}, u32[]{:S(2)}, u32[]{:S(2)}) async-start(bf16[8,320,128]{2,1,0:T(8,128)(2,1)} %shard_map.96.rest_0_), calls=%async_computation.3 | async-start | bytes 1310720 | tf_op jit(solution)/shard_map/all_to_all | solution.py:376
  188.9 1.7 collective-permute-start.13
  197.9 21.7 %all-to-all-start.5 = ((bf16[8,320,128]{2,1,0:T(8,128)(2,1)}), bf16[8,320,128]{2,1,0:T(8,128)(2,1)S(1)}, u32[]{:S(2)}, u32[]{:S(2)}) async-start(bf16[8,320,128]{2,1,0:T(8,128)(2,1)} %shard_map.99), calls=%async_computation.5 | async-start | bytes 1310720 | tf_op jit(solution)/shard_map/all_to_all | solution.py:376
  225.7 22.4 %collective-permute-start.14 = (bf16[320,1536]{1,0:T(8,128)(2,1)S(1)}, bf16[320,1536]{1,0:T(8,128)(2,1)S(1)}, u32[]{:S(2)}, u32[]{:S(2)}) collective-permute-start(bf16[320,1536]{1,0:T(8,128)(2,1)S(1)} %shard_map.101), channel_id=1, source_target_pairs={{0,1},{1,0},{2,3},{3,2},{4,5},{5,4},{6,7},{7,6},{8,9},{9,8},{10,11... | collective-permute-start | bytes 2949128 | tf_op jit(solution)/shard_map/ppermute | solution.py:463
  231.0 18.3 %copy-start.1 = (bf16[8,3072]{1,0:T(8,128)(2,1)S(1)}, bf16[8,3072]{1,0:T(8,128)(2,1)}, u32[]{:S(2)}) copy-start(bf16[8,3072]{1,0:T(8,128)(2,1)} %param.13) | copy-start | bytes 147460
  (7 other events, 13.6 us)
